TPU v7x, 256 devices: a whole 4x4x8 slice. The times are simulated.
256 devices in a mesh: tm: 64 (over x, z, core), chan: 4 (over y).
Axes of the slice: x: 4, y: 4, z: 8, core: 2. Of those that a mesh axis runs over, the one named last changes fastest.
Arguments:
- filterbank: bfloat16 [4096, 262144], P(('chan', 'tm')), may hold values from -6 to 6
- channel_mask: int32 [4096], P(('chan', 'tm')), may hold values 0 or 1
- delays: int32 [32, 64], P(None, 'chan'), may hold values from 0 to 127
- readers: int32 [2048, 8, 1], P('tm'), may hold values from 0 to 63; in each aligned block of 256 rows (0 to 255, 256 to 511, ..., all dimensions but the last counted through in order) at most 8 rows name the same one
- stretch: float32 [8], replicated, may hold values from 0.5 to 1.8
Outputs:
- series: bfloat16 [32, 262144], P('chan', 'tm')
- stacked: bfloat16 [8, 32, 8192], P(None, 'chan', 'tm')
Inputs may be any that keep to these rules, and one draw needn't show every extreme that they name: `readers`: among the 256 entries of the 32 blocks of one index of tm, no reader appears more than 8 times, and some reader appears exactly 8 times.
All inputs are finite; a program needn't handle non-finite values. No bound on the sum of `channel_mask` on one device may be relied on, other than what follows from the above.
Results may differ from a plain program's by a relative error of at most 0.0068.
Values may be sent and summed in bfloat16 or wider, within the bound.
A program may use at most 64 MiB of HBM per device.

v0:
```python
import math

import jax
import jax.numpy as jnp
from jax import lax
from jax.sharding import PartitionSpec as P

SUBCH = 64
BLK = 128


start_offset = 4.0
taper_half = 8.0


def from_behind(block, axis, distance):
    devices = range(lax.axis_size(axis))
    route = [(i - distance, i) for i in devices if i - distance in devices]
    return lax.ppermute(block, axis, route)


def sinc_table(stretch, width):
    row_pos = jnp.arange(2 * width, dtype=jnp.float32)[None, :, None]
    col_pos = jnp.arange(width, dtype=jnp.float32)[None, None, :]
    spread = row_pos - (start_offset + col_pos * stretch[:, None, None])
    taper = jnp.where(
        jnp.abs(spread) < taper_half, 0.5 + 0.5 * jnp.cos(math.pi * spread / taper_half), 0.0
    )
    return (jnp.sinc(spread) * taper).astype(jnp.bfloat16)


def on_device(filterbank, channel_mask, delays, readers, stretch):
    chan_dev, time_total = filterbank.shape
    tm_count = lax.axis_size("tm")
    time_dev = time_total // tm_count
    masked = filterbank * channel_mask.astype(jnp.bfloat16)[:, None]
    turned = lax.all_to_all(masked, "tm", split_axis=1, concat_axis=0, tiled=True)
    turned_rows = turned.shape[0]
    band_count = turned_rows // SUBCH
    selector = (
        jnp.arange(band_count)[:, None] == (jnp.arange(turned_rows) // SUBCH)[None, :]
    ).astype(jnp.bfloat16)
    sub_sum = jnp.dot(selector, turned, preferred_element_type=jnp.float32)
    sub = sub_sum.astype(jnp.bfloat16)
    sub_next = from_behind(sub[:, :BLK], "tm", -1)
    extended = jnp.concatenate([sub, sub_next], axis=1)
    block_count = time_dev // BLK
    band_blocks = extended.reshape(band_count, block_count + 1, BLK)
    lower_blocks = band_blocks[:, :-1]
    upper_blocks = band_blocks[:, 1:]
    row_index = jnp.arange(BLK, dtype=jnp.int32)[None, :, None]
    column_index = jnp.arange(BLK, dtype=jnp.int32)[None, None, :]

    def one_trial(delay_row):
        delay_cube = delay_row[:, None, None]
        near_tile = (row_index == column_index + delay_cube).astype(jnp.bfloat16)
        far_tile = (row_index + BLK == column_index + delay_cube).astype(jnp.bfloat16)
        subband_totals = jnp.einsum(
            "kbj,kji->bi", lower_blocks, near_tile, preferred_element_type=jnp.float32
        )
        subband_totals = subband_totals + jnp.einsum(
            "kbj,kji->bi", upper_blocks, far_tile, preferred_element_type=jnp.float32
        )
        return subband_totals.reshape(time_dev)

    dm_dev = delays.shape[0] // lax.axis_size("chan")
    series_sum = lax.psum_scatter(
        lax.map(one_trial, delays), "chan", scatter_dimension=0, tiled=True
    )
    series = series_sum.astype(jnp.bfloat16)
    series_next = from_behind(series[:, :BLK], "tm", -1)
    series_blocks = jnp.concatenate([series, series_next], axis=1).reshape(
        dm_dev, block_count + 1, BLK
    )
    window_slices = jnp.concatenate([series_blocks[:, :-1], series_blocks[:, 1:]], axis=2)
    resample_kernel = sinc_table(stretch, BLK)
    accel_count = stretch.shape[0]
    item_count = block_count * accel_count
    route = readers.reshape(item_count)
    capacity = max(2, 2 * item_count // tm_count)
    reader_hits = (route[:, None] == jnp.arange(tm_count, dtype=jnp.int32)[None, :]).astype(
        jnp.int32
    )
    earlier_hits = jnp.cumsum(reader_hits, axis=0) - reader_hits
    slot_index = jnp.sum(earlier_hits * reader_hits, axis=1)
    target_slot = route * capacity + slot_index
    slot_table = jnp.arange(tm_count * capacity, dtype=jnp.int32)[:, None] == target_slot[None, :]
    accel_of_item = jnp.arange(item_count, dtype=jnp.int32) % accel_count
    accel_tag = jnp.sum(jnp.where(slot_table, accel_of_item[None, :] + 1, 0), axis=1) - 1
    block_table = jnp.any(
        slot_table.reshape(tm_count * capacity, block_count, accel_count), axis=2
    ).astype(jnp.bfloat16)
    window_rows = jnp.transpose(window_slices, (1, 0, 2)).reshape(block_count, dm_dev * 2 * BLK)
    outgoing = jnp.dot(block_table, window_rows, preferred_element_type=jnp.float32).astype(
        jnp.bfloat16
    )
    arrived, arrived_tags = (
        lax.all_to_all(outgoing, "tm", split_axis=0, concat_axis=0, tiled=True),
        lax.all_to_all(accel_tag, "tm", split_axis=0, concat_axis=0, tiled=True),
    )
    arrived = arrived.reshape(-1, dm_dev, 2 * BLK)

    def one_accel(acceleration_position):
        stretched_series = jnp.einsum(
            "sdj,ji->sdi",
            arrived,
            resample_kernel[acceleration_position],
            preferred_element_type=jnp.float32,
        ).astype(jnp.bfloat16)
        selector_row = (arrived_tags == acceleration_position).astype(jnp.bfloat16)
        return jnp.einsum(
            "s,sdi->di", selector_row, stretched_series, preferred_element_type=jnp.float32
        )

    stacked = lax.map(one_accel, jnp.arange(accel_count, dtype=jnp.int32))
    return (series, stacked.astype(jnp.bfloat16))


def solution(mesh):
    return jax.shard_map(
        on_device,
        mesh=mesh,
        in_specs=(
            P(("chan", "tm"), None),
            P(("chan", "tm")),
            P(None, "chan"),
            P("tm", None, None),
            P(),
        ),
        out_specs=(P("chan", "tm"), P(None, "chan", "tm")),
        check_vma=False,
    )
```

profile of v0, /device:TPU:1, one launch (start us, length us, event | category | flops | bytes accessed | tf_op | source)
XLA Modules:
  0.0 446.0 jit_solution(2370082805119986184)
XLA Ops:
  7.8 7.2 %broadcast_multiply_fusion = bf16[16,262144]{1,0:T(8,128)(2,1)} fusion(bf16[16,262144]{1,0:T(8,128)(2,1)} %param.9, bf16[16]{0:T(256)(128)(2,1)S(1)} %convert_element_type.41), kind=kLoop, calls=%fused_computation.21 | loop fusion | flops 4194304 | bytes 16777248 | tf_op jit(solution)/shard_map/mul | solution.py:36
  15.0 7.7 %copy.49 = bf16[2,64,8,4096]{3,2,0,1:T(8,128)(2,1)} copy(bf16[2,64,8,4096]{3,2,1,0:T(8,128)(2,1)} %bitcast.103) | data formatting | bytes 16777216 | tf_op jit(solution)/shard_map/all_to_all | solution.py:37
  22.7 13.2 %all-to-all-start = ((bf16[16,64,4096]{2,0,1:T(8,128)(2,1)}), bf16[16,64,4096]{2,0,1:T(8,128)(2,1)}, u32[]{:S(2)}, u32[]{:S(2)}) async-start(bf16[16,64,4096]{2,0,1:T(8,128)(2,1)} %bitcast.104), calls=%async_computation | async-start | bytes 16777216 | tf_op jit(solution)/shard_map/all_to_all | solution.py:37
  36.0 185.7 %all-to-all-done = bf16[16,64,4096]{2,0,1:T(8,128)(2,1)} async-done(((bf16[16,64,4096]{2,0,1:T(8,128)(2,1)}), bf16[16,64,4096]{2,0,1:T(8,128)(2,1)}, u32[]{:S(2)}, u32[]{:S(2)}) %all-to-all-start) | async-done | bytes 8388640 | tf_op jit(solution)/shard_map/all_to_all | solution.py:37
  221.7 4.6 %convolution_convert_fusion.1 = bf16[16,4096]{1,0:T(8,128)(2,1)S(1)} fusion(bf16[1024,4096]{1,0:T(8,128)(2,1)} %bitcast.9, s32[1024]{0:T(1024)S(1)} %add_select_fusion), kind=kOutput, calls=%fused_computation.20 | convolution fusion | flops 134299648 | bytes 8523776 | tf_op jit(solution)/shard_map/dot_general | solution.py:43
  226.3 1.9 collective-permute-start
  228.5 2.7 collective-permute-done
  231.3 75.3 %while.23 = (s32[]{:T(128)}, f32[32,4096]{1,0:T(8,128)}, s32[32,16]{1,0:T(8,128)S(1)}, bf16[16,32,128]{2,1,0:T(8,128)(2,1)S(1)}, bf16[16,32,128]{2,1,0:T(8,128)(2,1)S(1)}, /*index=5*/s32[]{:T(128)}, s32[]{:T(128)}) while((s32[]{:T(128)}, f32[32,4096]{1,0:T(8,128)}, s32[32,16]{1,0:T(8,128)S(1)}, ...), condition=%wide.region_1.2_spmd.clone.clone, body=%wide.region_0.1_spmd.clone.clone.sunk | while | flops 34084992 | bytes 369941 | solution.py:68
  232.1 1.6 dynamic_update_slice.14
  234.4 1.6 dynamic_update_slice.14
  236.8 1.6 dynamic_update_slice.14
  239.1 1.6 dynamic_update_slice.14
  241.5 1.6 dynamic_update_slice.14
  243.8 1.6 dynamic_update_slice.14
  246.1 1.6 dynamic_update_slice.14
  248.5 1.6 dynamic_update_slice.14
  250.8 1.6 dynamic_update_slice.14
  253.2 1.6 dynamic_update_slice.14
  255.5 1.6 dynamic_update_slice.14
  257.9 1.6 dynamic_update_slice.14
  260.2 1.6 dynamic_update_slice.14
  262.6 1.6 dynamic_update_slice.14
  265.0 1.6 dynamic_update_slice.14
  267.3 1.6 dynamic_update_slice.14
  269.7 1.6 dynamic_update_slice.14
  272.0 1.6 dynamic_update_slice.14
  274.4 1.6 dynamic_update_slice.14
  276.8 1.6 dynamic_update_slice.14
  279.1 1.6 dynamic_update_slice.14
  281.5 1.6 dynamic_update_slice.14
  283.8 1.6 dynamic_update_slice.14
  286.2 1.6 dynamic_update_slice.14
  288.6 1.6 dynamic_update_slice.14
  290.9 1.6 dynamic_update_slice.14
  293.3 1.6 dynamic_update_slice.14
  295.6 1.6 dynamic_update_slice.14
  298.0 1.6 dynamic_update_slice.14
  300.3 1.6 dynamic_update_slice.14
  302.7 1.6 dynamic_update_slice.14
  305.0 1.6 dynamic_update_slice.14
  307.9 0.7 sub.39
  308.6 5.8 %all-to-all-start.1 = ((s32[64,8,1]{1,2,0:T(1,128)}), s32[64,8,1]{1,2,0:T(1,128)S(1)}, u32[]{:S(2)}, u32[]{:S(2)}) async-start(s32[64,8,1]{1,2,0:T(1,128)} %bitcast.11), calls=%async_computation.2 | async-start | bytes 65536 | tf_op jit(solution)/shard_map/all_to_all | solution.py:99
  314.5 11.4 %reduce-scatter.2.cloned.1.call-done = f32[8,4096]{1,0:T(8,128)} async-done(((f32[32,4096]{1,0:T(8,128)}), f32[8,4096]{1,0:T(8,128)}) %reduce-scatter.2.cloned.1.call-update) | async-done | bytes 131088 | tf_op jit(solution)/shard_map/reduce_scatter | solution.py:67
  325.9 0.9 convert_element_type.43
  326.8 4.1 collective-permute-start.1
  331.1 2.2 collective-permute-done.1
  333.4 2.1 fusion.12
  335.5 9.3 %all-to-all-start.2 = ((bf16[64,8,2048]{2,1,0:T(8,128)(2,1)}), bf16[64,8,2048]{2,1,0:T(8,128)(2,1)S(1)}, u32[]{:S(2)}, u32[]{:S(2)}) async-start(bf16[64,8,2048]{2,1,0:T(8,128)(2,1)} %fusion.12), calls=%async_computation.3 | async-start | bytes 4194304 | tf_op jit(solution)/shard_map/all_to_all | solution.py:98
  344.9 5.2 %fusion.29 = bf16[8,256,128]{1,2,0:T(8,128)(2,1)S(1)} fusion(f32[8,128]{1,0:T(8,128)S(1)} %multiply_add_fusion.1), kind=kLoop, calls=%fused_computation.51 | loop fusion | flops 10747904 | bytes 528384 | tf_op jit(solution)/shard_map/convert_element_type | solution.py:29
  351.5 44.6 %all-to-all-done.2 = bf16[64,8,2048]{2,1,0:T(8,128)(2,1)S(1)} async-done(((bf16[64,8,2048]{2,1,0:T(8,128)(2,1)}), bf16[64,8,2048]{2,1,0:T(8,128)(2,1)S(1)}, u32[]{:S(2)}, u32[]{:S(2)}) %all-to-all-start.2) | async-done | bytes 2097184 | tf_op jit(solution)/shard_map/all_to_all | solution.py:98
  397.2 41.9 %while.22 = (s32[]{:T(128)}, bf16[8,8,128]{2,1,0:T(8,128)(2,1)}, s32[8]{0:T(128)S(1)}, s32[512]{0:T(512)S(1)}, bf16[8,256,128]{1,2,0:T(8,128)(2,1)S(1)}, /*index...) while((s32[]{:T(128)}, bf16[8,8,128]{2,1,0:T(8,128)(2,1)}, s32[8]{0:T(128)S(1)}, ...), condition=%wide.region_9.10_spmd, body=%wide.region_8.9_spmd.sunk | while | flops 270008832 | bytes 4276883 | solution.py:115
  400.0 0.8 convolution_convert_fusion.4
  400.8 0.7 broadcast_compare_fusion.2
  405.2 0.8 convolution_convert_fusion.4
  406.0 0.7 broadcast_compare_fusion.2
  410.4 0.8 convolution_convert_fusion.4
  411.3 0.7 broadcast_compare_fusion.2
  415.7 0.8 convolution_convert_fusion.4
  416.5 0.7 broadcast_compare_fusion.2
  420.9 0.8 convolution_convert_fusion.4
  426.2 0.8 convolution_convert_fusion.4
  427.0 0.7 broadcast_compare_fusion.2
  431.4 0.8 convolution_convert_fusion.4
  436.6 0.8 convolution_convert_fusion.4
  (242 shorter events, 43.3 us)
Async XLA Ops:
  22.7 199.0 %all-to-all-start = ((bf16[16,64,4096]{2,0,1:T(8,128)(2,1)}), bf16[16,64,4096]{2,0,1:T(8,128)(2,1)}, u32[]{:S(2)}, u32[]{:S(2)}) async-start(bf16[16,64,4096]{2,0,1:T(8,128)(2,1)} %bitcast.104), calls=%async_computation | async-start | bytes 16777216 | tf_op jit(solution)/shard_map/all_to_all | solution.py:37
  35.9 192.3 %copy-start.1 = (s32[32,16]{0,1:T(8,128)S(1)}, s32[32,16]{0,1:T(8,128)}, u32[]{:S(2)}) copy-start(s32[32,16]{0,1:T(8,128)} %param.11) | copy-start | bytes 6148
  35.9 192.4 %copy-start.2 = (s32[32,8,1]{0,2,1:T(1,128)S(1)}, s32[32,8,1]{0,2,1:T(1,128)}, u32[]{:S(2)}) copy-start(s32[32,8,1]{0,2,1:T(1,128)} %param.12) | copy-start | bytes 3076
  35.9 289.9 %reduce-scatter.2.cloned.1.call-start = ((), (), s32[]{:S(2)}) async-start(), calls=%async_computation.4 | async-start | bytes 655360 | tf_op jit(solution)/shard_map/reduce_scatter | solution.py:67
  226.2 118.6 %copy-start.3 = (f32[8]{0:T(128)S(1)}, f32[8]{0:T(128)}, u32[]{:S(2)}) copy-start(f32[8]{0:T(128)} %param.13) | copy-start | bytes 100
  226.3 4.9 %collective-permute-start = (bf16[16,128]{1,0:T(8,128)(2,1)S(1)}, bf16[16,128]{1,0:T(8,128)(2,1)S(1)}, u32[]{:S(2)}, u32[]{:S(2)}) collective-permute-start(bf16[16,128]{1,0:T(8,128)(2,1)S(1)} %slice.32), channel_id=1, source_target_pairs={{4,0},{8,4},{12,8},{16,12},{20,16},{24,20},{28,24},{32,28},{36,32}... | collective-permute-start | bytes 12296 | tf_op jit(solution)/shard_map/ppermute | solution.py:19
  308.6 26.9 %all-to-all-start.1 = ((s32[64,8,1]{1,2,0:T(1,128)}), s32[64,8,1]{1,2,0:T(1,128)S(1)}, u32[]{:S(2)}, u32[]{:S(2)}) async-start(s32[64,8,1]{1,2,0:T(1,128)} %bitcast.11), calls=%async_computation.2 | async-start | bytes 65536 | tf_op jit(solution)/shard_map/all_to_all | solution.py:99
  326.8 70.4 %copy-start = (bf16[8,4096]{1,0:T(8,128)(2,1)}, bf16[8,4096]{1,0:T(8,128)(2,1)S(1)}, u32[]{:S(2)}) copy-start(bf16[8,4096]{1,0:T(8,128)(2,1)S(1)} %convert_element_type.43) | copy-start | bytes 196612
  326.8 6.5 %collective-permute-start.1 = (bf16[8,128]{1,0:T(8,128)(2,1)S(1)}, bf16[8,128]{1,0:T(8,128)(2,1)S(1)}, u32[]{:S(2)}, u32[]{:S(2)}) collective-permute-start(bf16[8,128]{1,0:T(8,128)(2,1)S(1)} %slice.36), channel_id=1, source_target_pairs={{4,0},{8,4},{12,8},{16,12},{20,16},{24,20},{28,24},{32,28},{36,32}... | collective-permute-start | bytes 6152 | tf_op jit(solution)/shard_map/ppermute | solution.py:19
  335.5 60.6 %all-to-all-start.2 = ((bf16[64,8,2048]{2,1,0:T(8,128)(2,1)}), bf16[64,8,2048]{2,1,0:T(8,128)(2,1)S(1)}, u32[]{:S(2)}, u32[]{:S(2)}) async-start(bf16[64,8,2048]{2,1,0:T(8,128)(2,1)} %fusion.12), calls=%async_computation.3 | async-start | bytes 4194304 | tf_op jit(solution)/shard_map/all_to_all | solution.py:98
Sparse Core Ops, SparseCore 0:
  306.8 19.0 reduce-scatter.1
where the time goes:
time: 447 us; the launch traced here: 446 us
  waiting for transfers between devices  247 us (55%)
  local copies, waits for them, and re-layouts  72.9 us (16%)
  matrix products  36.4 us (8%)
  starting transfers between devices  34.3 us (8%)
  other arithmetic  24 us (5%)
  loops' own time  17.6 us (4%)
  between operations  14.3 us (3%)
    all_to_all x1, waiting for transfers between devices, on_device(): lax.all_to_all(masked, 'tm', split_axis=1, concat_axis=0, tiled=True)  186 us
    dynamic_update_slice x32, local copies, waits for them, and re-layouts, on_device(): lax.map(one_trial, delays)  51.6 us
    all_to_all x1, waiting for transfers between devices, on_device(): lax.all_to_all(outgoing, 'tm', split_axis=0, concat_axis=0, tiled=True)  44.6 us
    another operation x1, loops' own time, on_device(): stacked = lax.map(one_accel, jnp.arange(accel_count, dtype=jnp.int32))  16.8 us
    all_to_all x1, starting transfers between devices, on_device(): lax.all_to_all(masked, 'tm', split_axis=1, concat_axis=0, tiled=True)  13.2 us
    reduce_scatter x1, waiting for transfers between devices, on_device(): lax.psum_scatter(lax.map(one_trial, delays), 'chan', scatter_dimension=0,...  11.4 us
    dot_general x32, matrix products, one_trial(): jnp.einsum('kbj,kji->bi', upper_blocks, far_tile, preferred_element_type=...  11.2 us
    all_to_all x1, starting transfers between devices, on_device(): lax.all_to_all(outgoing, 'tm', split_axis=0, concat_axis=0, tiled=True)  9.3 us
  transfers between devices with their start and end apart: 6, of which 5 were waited for; matrix products, arithmetic and copies ran while one was open for 3% of the time, Pallas kernels for 0%

commit v1 on v0

v1 whole, which is shorter than its diff:
```python
import functools
import math

import jax
import jax.numpy as jnp
from jax import lax
from jax.experimental import pallas as pl
from jax.experimental.pallas import tpu as pltpu
from jax.sharding import PartitionSpec as P

MESH = pl.DeviceIdType.MESH
BF, F32 = jnp.bfloat16, jnp.float32

BLK = 128
N_TM = 64
N_CHAN = 4
SHARD = 4096
ROWS = SHARD // BLK
PAIRS = N_TM // 2
OWN = 16
TRIALS = 8
NSUB = 64
NX = 4
NQ = 16
NACC = 8
SENT = TRIALS * ROWS + 16
CHUNK = 4
START_OFFSET = 4.0
TAPER_HALF = 8.0


def remote(src, dst, send_sem, recv_sem, tm, chan):
    return pltpu.make_async_remote_copy(
        src_ref=src,
        dst_ref=dst,
        send_sem=send_sem,
        recv_sem=recv_sem,
        device_id=(tm, chan),
        device_id_type=MESH,
    )


def subband_kernel(
    fb, mask, delays,
    sub_all, halo_all, delays_all,
    fb_v, lhs_v, for_core, from_core, staged, parts, halo_f, halo_v,
    load_sem, core_send, core_recv, part_send, part_recv,
    sub_send, sub_recv, halo_send, halo_recv, delay_send, delay_recv,
):
    t, c = lax.axis_index("tm"), lax.axis_index("chan")
    core, me = t % 2, t // 2
    other = t + 1 - 2 * core

    def shard_at(n, parity):
        return 2 * ((me + 1 + n) % PAIRS) + parity

    def load(n, parity, slot):
        at = pl.ds(pl.multiple_of(shard_at(n, parity) * SHARD, SHARD), SHARD)
        return pltpu.make_async_copy(fb.at[:, at], fb_v.at[:, at], load_sem.at[slot])

    def start_other(n, carry):
        load(n, 1 - core, n).start()
        return carry

    def start_own(n, carry):
        load(n, core, PAIRS + n).start()
        return carry

    lax.fori_loop(0, PAIRS, start_other, 0)
    lax.fori_loop(0, PAIRS, start_own, 0)

    barrier = pltpu.get_barrier_semaphore()

    def greet(tm, chan):
        pl.semaphore_signal(barrier, inc=1, device_id=(tm, chan), device_id_type=MESH)

    def greet_plane(n, carry):
        greet(2 * ((me + 1 + n) % PAIRS) + core, c)
        return carry

    lax.fori_loop(0, PAIRS - 1, greet_plane, 0)
    for step in range(1, N_CHAN):
        greet(t, (c + step) % N_CHAN)

    @pl.when(t > 0)
    def _():
        for chan in range(N_CHAN):
            greet(t - 1, chan)

    @pl.when(t < N_TM - 1)
    def _():
        for chan in range(N_CHAN):
            greet(t + 1, chan)

    lane = lax.broadcasted_iota(jnp.int32, (16, 16 * OWN), 1)
    row = lax.broadcasted_iota(jnp.int32, (16, 16 * OWN), 0)
    weights = jnp.zeros((16, 16 * OWN), F32)
    for channel in range(OWN):
        value = mask[channel].astype(F32)
        weights = jnp.where((lane // OWN == row) & (lane % OWN == channel), value, weights)
    lhs_v[...] = weights.astype(BF)

    def shard_sum(shard):
        halves = []
        for half in range(2):
            at = pl.multiple_of(shard * SHARD + half * (SHARD // 2), SHARD // 2)
            block = fb_v[:, pl.ds(at, SHARD // 2)]
            halves.append(
                jnp.concatenate([block[:, i * BLK:(i + 1) * BLK] for i in range(16)], axis=0)
            )
        total = jnp.dot(
            lhs_v[...], jnp.concatenate(halves, axis=1), preferred_element_type=F32
        )
        return jnp.concatenate([total[:, :BLK], total[:, BLK:]], axis=0)

    def to_core(chunk):
        rows = pl.ds(chunk * CHUNK, CHUNK)
        return remote(
            for_core.at[rows], from_core.at[rows],
            core_send.at[chunk], core_recv.at[chunk], other, c,
        )

    pl.semaphore_wait(
        barrier,
        PAIRS - 1 + N_CHAN - 1
        + N_CHAN * (t > 0).astype(jnp.int32)
        + N_CHAN * (t < N_TM - 1).astype(jnp.int32),
    )

    def delay_copy(step):
        return remote(
            delays, delays_all.at[c], delay_send.at[step - 1], delay_recv.at[c],
            t, (c + step) % N_CHAN,
        )

    for step in range(1, N_CHAN):
        delay_copy(step).start()
    delays_all[c] = delays[...]

    def sum_other(chunk, carry):
        for i in range(CHUNK):
            n = chunk * CHUNK + i
            load(n, 1 - core, n).wait()
            for_core[n] = shard_sum(shard_at(n, 1 - core)).astype(BF)
        to_core(chunk).start()
        return carry

    lax.fori_loop(0, PAIRS // CHUNK, sum_other, 0)

    def send_part(n):
        return remote(
            staged.at[n], parts.at[me], part_send.at[n], part_recv.at[me],
            shard_at(n, core), c,
        )

    def sum_own(chunk, carry):
        to_core(chunk).wait_recv()
        for i in range(CHUNK):
            n = chunk * CHUNK + i
            load(n, core, PAIRS + n).wait()
            total = shard_sum(shard_at(n, core)) + from_core[n].astype(F32)
            staged[n] = total.astype(BF)

            @pl.when(n < PAIRS - 1)
            def _():
                send_part(n).start()

        return carry

    lax.fori_loop(0, PAIRS // CHUNK, sum_own, 0)
    parts[me] = staged[PAIRS - 1]

    def part_arrival(j):
        return remote(parts.at[j], parts.at[j], part_send.at[0], part_recv.at[j], other, c)

    for k in range(OWN):
        for j in (2 * k, 2 * k + 1):
            @pl.when(j != me)
            def _():
                part_arrival(j).wait_recv()
        total = parts[2 * k].astype(F32) + parts[2 * k + 1].astype(F32)
        sub_all[c, k * ROWS:(k + 1) * ROWS] = total.astype(BF)
        halo_f[2 * k:2 * k + 2] = total[:2]
    halo_v[...] = halo_f[...].astype(BF)

    def sub_copy(step):
        return remote(
            sub_all.at[c], sub_all.at[c], sub_send.at[step - 1], sub_recv.at[c],
            t, (c + step) % N_CHAN,
        )

    def halo_copy(chan):
        return remote(
            halo_v, halo_all.at[c], halo_send.at[chan], halo_recv.at[c], t - 1, chan
        )

    for step in (2, 1, 3):
        sub_copy(step).start()

    @pl.when(t > 0)
    def _():
        for chan in range(N_CHAN):
            halo_copy(chan).start()

    @pl.when(t == N_TM - 1)
    def _():
        halo_all[...] = jnp.zeros_like(halo_all)

    def sent_core(chunk, carry):
        to_core(chunk).wait_send()
        return carry

    def sent_part(n, carry):
        send_part(n).wait_send()
        return carry

    lax.fori_loop(0, PAIRS // CHUNK, sent_core, 0)
    lax.fori_loop(0, PAIRS - 1, sent_part, 0)
    for step in range(1, N_CHAN):
        delay_copy(step).wait_send()
        source = (c + step) % N_CHAN
        remote(
            delays, delays_all.at[source], delay_send.at[0], delay_recv.at[source], t, source
        ).wait_recv()

    @pl.when(t < N_TM - 1)
    def _():
        for chan in range(N_CHAN):
            remote(
                halo_v, halo_all.at[chan], halo_send.at[0], halo_recv.at[chan], t + 1, chan
            ).wait_recv()

    @pl.when(t > 0)
    def _():
        for chan in range(N_CHAN):
            halo_copy(chan).wait_send()

    for step in range(1, N_CHAN):
        source = (c + step) % N_CHAN
        remote(
            sub_all.at[source], sub_all.at[source], sub_send.at[0], sub_recv.at[source],
            t, source,
        ).wait_recv()
        sub_copy(step).wait_send()


def subbands(filterbank, channel_mask, delays):
    vmem = pl.BlockSpec(memory_space=pltpu.VMEM)
    dma = pltpu.SemaphoreType.DMA
    return pl.pallas_call(
        subband_kernel,
        out_shape=(
            jax.ShapeDtypeStruct((N_CHAN, OWN * ROWS, BLK), BF),
            jax.ShapeDtypeStruct((N_CHAN, 2 * OWN, BLK), BF),
            jax.ShapeDtypeStruct((N_CHAN,) + delays.shape, jnp.int32),
        ),
        in_specs=[
            pl.BlockSpec(memory_space=pl.ANY),
            pl.BlockSpec(memory_space=pltpu.SMEM),
            vmem,
        ],
        out_specs=(vmem, vmem, vmem),
        scratch_shapes=[
            pltpu.VMEM(filterbank.shape, BF),
            pltpu.VMEM((16, 16 * OWN), BF),
            pltpu.VMEM((PAIRS, ROWS, BLK), BF),
            pltpu.VMEM((PAIRS, ROWS, BLK), BF),
            pltpu.VMEM((PAIRS, ROWS, BLK), BF),
            pltpu.VMEM((PAIRS, ROWS, BLK), BF),
            pltpu.VMEM((2 * OWN, BLK), F32),
            pltpu.VMEM((2 * OWN, BLK), BF),
            dma((N_TM,)),
            dma((PAIRS // CHUNK,)),
            dma((PAIRS // CHUNK,)),
            dma((PAIRS,)),
            dma((PAIRS,)),
            dma((N_CHAN,)),
            dma((N_CHAN,)),
            dma((N_CHAN,)),
            dma((N_CHAN,)),
            dma((N_CHAN,)),
            dma((N_CHAN,)),
        ],
        compiler_params=pltpu.CompilerParams(
            collective_id=0, has_side_effects=True, vmem_limit_bytes=24 * 2**20
        ),
        name="subbands",
    )(filterbank, channel_mask, delays)


def dedisperse_kernel(sub_all, halo_all, delays_all, series, rows, wide, halo_f, turned, halo_rows):
    c = lax.axis_index("chan")
    for chan in range(N_CHAN):
        halo_f[chan] = halo_all[chan].astype(F32)
    for k in range(NSUB):
        chan, own = k // OWN, k % OWN
        wide[k, :ROWS] = sub_all[chan, own * ROWS:(own + 1) * ROWS].astype(F32)
        wide[k, ROWS:ROWS + 2] = halo_f[chan, 2 * own:2 * own + 2]
    lane = lax.broadcasted_iota(jnp.int32, (1, BLK), 1)
    tall = ROWS + 8

    def one_band(k, totals):
        lower = wide[k, 0:tall]
        upper = wide[k, 1:tall + 1]
        out = []
        for m in range(TRIALS):
            delay = delays_all[k // OWN, c * TRIALS + m, k % OWN]
            joined = jnp.where(lane >= delay, lower, upper)
            out.append(totals[m] + pltpu.roll(joined, (BLK - delay) % BLK, 1))
        return tuple(out)

    totals = lax.fori_loop(
        0, NSUB, one_band, tuple(jnp.zeros((tall, BLK), F32) for _ in range(TRIALS))
    )
    halo_rows[...] = jnp.zeros_like(halo_rows)
    for m in range(TRIALS):
        rows[m * ROWS:(m + 1) * ROWS] = totals[m][:ROWS].astype(BF)
        halo_rows[m:m + 1] = totals[m][ROWS:ROWS + 1]
        turned[pl.ds(m, ROWS, stride=TRIALS)] = totals[m][:ROWS]
    rows[TRIALS * ROWS:] = halo_rows[...].astype(BF)
    for b in range(ROWS):
        series[:, b * BLK:(b + 1) * BLK] = turned[b * TRIALS:(b + 1) * TRIALS].astype(BF)


def dedisperse(sub_all, halo_all, delays_all):
    vmem = pl.BlockSpec(memory_space=pltpu.VMEM)
    return pl.pallas_call(
        dedisperse_kernel,
        out_shape=(
            jax.ShapeDtypeStruct((TRIALS, SHARD), BF),
            jax.ShapeDtypeStruct((SENT, BLK), BF),
        ),
        in_specs=[vmem, vmem, pl.BlockSpec(memory_space=pltpu.SMEM)],
        out_specs=(vmem, vmem),
        scratch_shapes=[
            pltpu.VMEM((NSUB, ROWS + 16, BLK), F32),
            pltpu.VMEM((N_CHAN, 2 * OWN, BLK), F32),
            pltpu.VMEM((TRIALS * ROWS, BLK), F32),
            pltpu.VMEM((16, BLK), F32),
        ],
        compiler_params=pltpu.CompilerParams(vmem_limit_bytes=16 * 2**20),
        name="dedisperse",
    )(sub_all, halo_all, delays_all)


def sinc_table(stretch_value):
    col = lax.broadcasted_iota(jnp.int32, (8, BLK), 1).astype(F32)
    centre = START_OFFSET + col * stretch_value
    whole = jnp.round(centre)
    odd = whole - 2.0 * jnp.floor(whole * 0.5)
    wave = (2.0 * odd - 1.0) * jnp.sin(math.pi * (centre - whole)) / math.pi
    angle = (math.pi / TAPER_HALF) * (centre - 16.0 * jnp.floor(centre / 16.0))
    cos_p, sin_p = 0.5 * jnp.cos(angle), 0.5 * jnp.sin(angle)
    pieces = []
    row = lax.broadcasted_iota(jnp.int32, (8, BLK), 0)
    sign = (1 - 2 * (row % 2)).astype(F32)
    signed_wave = sign * wave
    tapers = []
    for half in range(2):
        turn = (math.pi / TAPER_HALF) * (row + 8 * half).astype(F32)
        tapers.append(0.5 + jnp.cos(turn) * cos_p + jnp.sin(turn) * sin_p)
    for group in range(2 * BLK // 8):
        x = (row + 8 * group).astype(F32) - centre
        sinc = jnp.where(x == 0.0, 1.0, signed_wave / jnp.where(x == 0.0, 1.0, x))
        pieces.append(jnp.where(jnp.abs(x) < TAPER_HALF, sinc * tapers[group % 2], 0.0))
    return jnp.concatenate(pieces, axis=0).astype(BF)


def stack_kernel(
    rows, readers, stretch,
    stacked,
    gathered, readers_all, table, tall, grouped, outgoing, arrived,
    row_send, row_recv, reader_send, reader_recv, out_send, out_recv,
):
    t, c = lax.axis_index("tm"), lax.axis_index("chan")
    x, q = t // NQ, t % NQ
    barrier = pltpu.get_barrier_semaphore()

    def greet(tm):
        pl.semaphore_signal(barrier, inc=1, device_id=(tm, c), device_id_type=MESH)

    for step in range(1, NX):
        greet(((x + step) % NX) * NQ + q)
    for step in range(1, NQ):
        greet(x * NQ + (q + step) % NQ)
    pl.semaphore_wait(barrier, NX - 1 + NQ - 1)

    def row_copy(step):
        return remote(
            rows, gathered.at[x], row_send.at[step - 1], row_recv.at[x],
            ((x + step) % NX) * NQ + q, c,
        )

    def reader_copy(step):
        return remote(
            readers, readers_all.at[x], reader_send.at[step - 1], reader_recv.at[x],
            ((x + step) % NX) * NQ + q, c,
        )

    for step in (2, 1, 3):
        row_copy(step).start()
    for step in (2, 1, 3):
        reader_copy(step).start()
    gathered[x] = rows[...]
    readers_all[x] = readers[...]

    def one_table(a, carry):
        table[a] = sinc_table(stretch[a])
        return carry

    lax.fori_loop(0, NACC, one_table, 0)

    for step in range(1, NX):
        source = (x + step) % NX
        remote(
            readers, readers_all.at[source], reader_send.at[0], reader_recv.at[source],
            source * NQ + q, c,
        ).wait_recv()
    lane = lax.broadcasted_iota(jnp.int32, (ROWS, BLK), 1)
    chosen = []
    for source in range(NX):
        names = readers_all[source]
        wanted = jnp.zeros((ROWS, BLK), jnp.int32)
        for a in range(NACC):
            wanted = jnp.where(lane // NQ == a, names[:, a:a + 1], wanted)
        chosen.append((wanted == x * NQ + lane % NQ).astype(F32))
    pick = jnp.concatenate(chosen, axis=0).T.astype(BF)

    for step in range(1, NX):
        source = (x + step) % NX
        remote(
            rows, gathered.at[source], row_send.at[0], row_recv.at[source],
            source * NQ + q, c,
        ).wait_recv()
    for source in range(NX):
        last = gathered[source, TRIALS * ROWS:].astype(F32)
        for m in range(TRIALS):
            tall[m, source, :ROWS] = gathered[source, m * ROWS:(m + 1) * ROWS].astype(F32)
            tall[m, source, ROWS:ROWS + 1] = last[m:m + 1]
    for m in range(TRIALS):
        for half in range(2):
            block = jnp.concatenate(
                [tall[m, source, half:half + ROWS] for source in range(NX)], axis=0
            ).astype(BF)
            sums = jnp.dot(pick, block, preferred_element_type=F32)
            for a in range(NACC):
                grouped[a, half, pl.ds(m, NQ, stride=TRIALS)] = sums[a * NQ:(a + 1) * NQ]

    def two_accelerations(pair, carry):
        results = []
        for i in range(2):
            a = 2 * pair + i
            block = jnp.concatenate([grouped[a, 0], grouped[a, 1]], axis=1).astype(BF)
            results.append(jnp.dot(block, table[a], preferred_element_type=F32))
        for reader in range(NQ):
            at = slice(reader * TRIALS, (reader + 1) * TRIALS)
            outgoing[reader, pl.ds(pl.multiple_of(pair * 16, 16), 16)] = jnp.concatenate(
                [results[0][at], results[1][at]], axis=0
            ).astype(BF)
        return carry

    lax.fori_loop(0, NACC // 2, two_accelerations, 0)

    def out_copy(step):
        target = (q + step) % NQ
        return remote(
            outgoing.at[target], arrived.at[q], out_send.at[step - 1], out_recv.at[q],
            x * NQ + target, c,
        )

    for step in range(1, NQ):
        out_copy(step).start()
    total = outgoing[q].astype(F32)
    for step in range(1, NQ):
        source = (q + step) % NQ
        remote(
            outgoing.at[0], arrived.at[source], out_send.at[0], out_recv.at[source],
            x * NQ + source, c,
        ).wait_recv()
        total = total + arrived[source].astype(F32)
    for a in range(NACC):
        stacked[a] = total[a * TRIALS:(a + 1) * TRIALS].astype(BF)
    for step in range(1, NQ):
        out_copy(step).wait_send()
    for step in range(1, NX):
        row_copy(step).wait_send()
        reader_copy(step).wait_send()


def stack(rows, readers, stretch):
    vmem = pl.BlockSpec(memory_space=pltpu.VMEM)
    dma = pltpu.SemaphoreType.DMA
    return pl.pallas_call(
        stack_kernel,
        out_shape=jax.ShapeDtypeStruct((NACC, TRIALS, BLK), BF),
        in_specs=[vmem, vmem, pl.BlockSpec(memory_space=pltpu.SMEM)],
        out_specs=vmem,
        scratch_shapes=[
            pltpu.VMEM((NX, SENT, BLK), BF),
            pltpu.VMEM((NX, ROWS, NACC), jnp.int32),
            pltpu.VMEM((NACC, 2 * BLK, BLK), BF),
            pltpu.VMEM((TRIALS, NX, ROWS + 8, BLK), F32),
            pltpu.VMEM((NACC, 2, TRIALS * NQ, BLK), F32),
            pltpu.VMEM((NQ, NACC * TRIALS, BLK), BF),
            pltpu.VMEM((NQ, NACC * TRIALS, BLK), BF),
            dma((NX,)),
            dma((NX,)),
            dma((NX,)),
            dma((NX,)),
            dma((NQ,)),
            dma((NQ,)),
        ],
        compiler_params=pltpu.CompilerParams(
            collective_id=1, has_side_effects=True, vmem_limit_bytes=16 * 2**20
        ),
        name="stack",
    )(rows, readers, stretch)


def on_device(filterbank, channel_mask, delays, readers, stretch):
    sub_all, halo_all, delays_all = subbands(filterbank, channel_mask, delays)
    series, rows = dedisperse(sub_all, halo_all, delays_all)
    stacked = stack(rows, readers.reshape(ROWS, NACC), stretch)
    return series, stacked


def solution(mesh):
    return jax.shard_map(
        on_device,
        mesh=mesh,
        in_specs=(
            P(("chan", "tm"), None),
            P(("chan", "tm")),
            P(None, "chan"),
            P("tm", None, None),
            P(),
        ),
        out_specs=(P("chan", "tm"), P(None, "chan", "tm")),
        check_vma=False,
    )
```

time: 447 us -> 78.9 us (0.18)
  waiting for transfers between devices: 247 us -> 0 us
  Pallas kernels: 0 us -> 72.6 us
  local copies, waits for them, and re-layouts: 72.9 us -> 5.51 us
  matrix products: 36.4 us -> 0 us
  starting transfers between devices: 34.3 us -> 0 us
  other arithmetic: 24 us -> 0 us
  loops' own time: 17.6 us -> 0 us
  between operations: 14.3 us -> 0.67 us
    all_to_all x3 -> x0, waiting for transfers between devices: 230 us -> none  [the longest x1 186 us: on_device(): lax.all_to_all(masked, 'tm', split_axis=1, concat_axis=0, tiled=True)]
    pallas_call x0 -> x3, Pallas kernels: none -> 72.6 us  [the longest x1 41.8 us: subbands(): pl.pallas_call(subband_kernel, out_shape=(jax.ShapeDtypeStruct((N_CHAN, O...]
    dynamic_update_slice x40 -> x0, local copies, waits for them, and re-layouts: 56.4 us -> none  [the longest x32 51.6 us: on_device(): lax.map(one_trial, delays)]
    dot_general x74 -> x0, matrix products: 33.4 us -> none  [the longest x32 11.2 us: one_trial(): jnp.einsum('kbj,kji->bi', upper_blocks, far_tile, preferred_element_type=...]
    all_to_all x3 -> x0, starting transfers between devices: 28.3 us -> none  [the longest x1 13.2 us: on_device(): lax.all_to_all(masked, 'tm', split_axis=1, concat_axis=0, tiled=True)]
    another operation x2 -> x0, loops' own time: 17.6 us -> none  [the longest x1 16.8 us: on_device(): stacked = lax.map(one_accel, jnp.arange(accel_count, dtype=jnp.int32))]
    reduce_scatter x1 -> x0, waiting for transfers between devices: 11.4 us -> none  [on_device(): lax.psum_scatter(lax.map(one_trial, delays), 'chan', scatter_dimension=0,...]
    all_to_all x3 -> x0, local copies, waits for them, and re-layouts: 8.34 us -> none  [the longest x1 7.71 us: on_device(): lax.all_to_all(masked, 'tm', split_axis=1, concat_axis=0, tiled=True)]
  transfers between devices with their start and end apart: 6 -> 0, of which waited for: 5 -> 0; matrix products, arithmetic and copies ran while one was open for 3% -> 0% of each run, Pallas kernels for 0% -> 0%
where the time goes in v1:
time: 78.9 us; the launch traced here: 78.8 us
  Pallas kernels  72.6 us (92%)
  local copies, waits for them, and re-layouts  5.51 us (7%)
    pallas_call x1, Pallas kernels, subbands(): pl.pallas_call(subband_kernel, out_shape=(jax.ShapeDtypeStruct((N_CHAN, O...  41.8 us
    pallas_call x1, Pallas kernels, stack(): pl.pallas_call(stack_kernel, out_shape=jax.ShapeDtypeStruct((NACC, TRIALS...  20.7 us
    pallas_call x1, Pallas kernels, dedisperse(): pl.pallas_call(dedisperse_kernel, out_shape=(jax.ShapeDtypeStruct((TRIALS...  10.1 us
    unnamed x11, local copies, waits for them, and re-layouts  5.51 us

profile of v1, /device:TPU:1, one launch (start us, length us, event | category | flops | bytes accessed | tf_op | source)
XLA Modules:
  0.0 78.8 jit_solution(1139775816975550112)
XLA Ops:
  0.6 0.0 copy-start.3
  0.6 0.0 copy-start.2
  0.7 0.8 copy.7.delays
  1.4 0.0 copy-start
  1.4 3.4 %copy-done = bf16[16,262144]{1,0:T(8,128)(2,1)S(1)} copy-done((bf16[16,262144]{1,0:T(8,128)(2,1)S(1)}, bf16[16,262144]{1,0:T(8,128)(2,1)}, u32[]{:S(2)}) %copy-start) | copy-done | bytes 8388632
  4.8 0.0 copy-start.1
  4.8 0.7 copy-done.1
  5.5 41.8 %subbands.1 = (bf16[4,512,128]{2,1,0:T(8,128)(2,1)S(1)}, bf16[4,32,128]{2,1,0:T(8,128)(2,1)S(1)}, s32[4,32,16]{2,1,0:T(8,128)S(1)}) custom-call(bf16[16,262144]{1,0:T(8,128)(2,1)S(1)} %copy-done, s32[16]{0:T(128)S(1)} %copy-done.1, s32[32,16]{1,0:T(8,128)S(1)} %copy.7.delays), custom_call_target="tpu_custom_call" | custom-call | tf_op jit(solution)/shard_map/subbands/pallas_call | solution.py:250
  47.3 10.1 %dedisperse.1 = (bf16[8,4096]{1,0:T(8,128)(2,1)}, bf16[272,128]{1,0:T(8,128)(2,1)S(1)}) custom-call(bf16[4,512,128]{2,1,0:T(8,128)(2,1)S(1)} %get-tuple-element.7.sub_all, bf16[4,32,128]{2,1,0:T(8,128)(2,1)S(1)} %get-tuple-element.8.halo_all, s32[4,32,16]{2,1,0:T(8,128)S(1)} %get-tuple-element.9.delays_all), custom_call_target="tpu_custom_call" | custom-call | tf_op jit(solution)/shard_map/dedisperse/pallas_call | solution.py:327
  57.4 0.0 copy-done.3
  57.4 0.1 copy.8
  57.5 0.0 copy-done.2
  57.5 20.7 %stack.1 = bf16[8,8,128]{2,1,0:T(8,128)(2,1)S(1)} custom-call(bf16[272,128]{1,0:T(8,128)(2,1)S(1)} %get-tuple-element.11.rows, s32[32,8]{1,0:T(8,128)S(1)} %bitcast.1, f32[8]{0:T(128)S(1)} %copy-done.2), custom_call_target="tpu_custom_call" | custom-call | tf_op jit(solution)/shard_map/stack/pallas_call | solution.py:493
  78.2 0.6 copy.10
Async XLA Ops:
  0.6 56.8 %copy-start.3 = (s32[32,8,1]{0,2,1:T(1,128)S(1)}, s32[32,8,1]{0,2,1:T(1,128)}, u32[]{:S(2)}) copy-start(s32[32,8,1]{0,2,1:T(1,128)} %param.8) | copy-start | bytes 3076
  0.6 56.8 %copy-start.2 = (f32[8]{0:T(128)S(1)}, f32[8]{0:T(128)}, u32[]{:S(2)}) copy-start(f32[8]{0:T(128)} %stretch.1) | copy-start | bytes 100
  1.4 3.4 %copy-start = (bf16[16,262144]{1,0:T(8,128)(2,1)S(1)}, bf16[16,262144]{1,0:T(8,128)(2,1)}, u32[]{:S(2)}) copy-start(bf16[16,262144]{1,0:T(8,128)(2,1)} %fb.1) | copy-start | bytes 25165828
  4.8 0.7 copy-start.1

commit v2 on v1

v2 whole, which is shorter than its diff:
```python
import math

import jax
import jax.numpy as jnp
from jax import lax
from jax.experimental import pallas as pl
from jax.experimental.pallas import tpu as pltpu
from jax.sharding import PartitionSpec as P

MESH = pl.DeviceIdType.MESH
BF, F32 = jnp.bfloat16, jnp.float32

BLK = 128
N_TM = 64
N_CHAN = 4
SHARD = 4096
ROWS = SHARD // BLK
PAIRS = N_TM // 2
OWN = 16
TRIALS = 8
NX = 4
NQ = 16
NACC = 8
GROUP = 32
LANE_GROUPS = BLK // GROUP
STEPS = 4
REACH = GROUP * (STEPS + 1)
CHUNK = 4
START_OFFSET = 4.0
TAPER_HALF = 8.0


def remote(src, dst, send_sem, recv_sem, tm, chan):
    return pltpu.make_async_remote_copy(
        src_ref=src,
        dst_ref=dst,
        send_sem=send_sem,
        recv_sem=recv_sem,
        device_id=(tm, chan),
        device_id_type=MESH,
    )


def sinc_table(stretch_value):
    col = lax.broadcasted_iota(jnp.int32, (8, BLK), 1).astype(F32)
    centre = START_OFFSET + col * stretch_value
    whole = jnp.round(centre)
    odd = whole - 2.0 * jnp.floor(whole * 0.5)
    wave = (2.0 * odd - 1.0) * jnp.sin(math.pi * (centre - whole)) / math.pi
    angle = (math.pi / TAPER_HALF) * (centre - 16.0 * jnp.floor(centre / 16.0))
    cos_p, sin_p = 0.5 * jnp.cos(angle), 0.5 * jnp.sin(angle)
    pieces = []
    row = lax.broadcasted_iota(jnp.int32, (8, BLK), 0)
    sign = (1 - 2 * (row % 2)).astype(F32)
    signed_wave = sign * wave
    tapers = []
    for half in range(2):
        turn = (math.pi / TAPER_HALF) * (row + 8 * half).astype(F32)
        tapers.append(0.5 + jnp.cos(turn) * cos_p + jnp.sin(turn) * sin_p)
    for group in range(2 * BLK // 8):
        x = (row + 8 * group).astype(F32) - centre
        sinc = jnp.where(x == 0.0, 1.0, signed_wave / jnp.where(x == 0.0, 1.0, x))
        pieces.append(jnp.where(jnp.abs(x) < TAPER_HALF, sinc * tapers[group % 2], 0.0))
    return jnp.concatenate(pieces, axis=0).astype(BF)


def turn(blocks):
    lane_group = lax.broadcasted_iota(jnp.int32, (ROWS, BLK), 1) // GROUP
    stacked = []
    for g in range(LANE_GROUPS):
        merged = blocks[0]
        for i in range(LANE_GROUPS):
            shift = (i - g) * GROUP % BLK
            moved = pltpu.roll(blocks[i], shift, 1) if shift else blocks[i]
            merged = moved if i == 0 else jnp.where(lane_group == i, moved, merged)
        stacked.append(merged)
    return jnp.concatenate(stacked, axis=0).T


def turn_back(rows):
    lane_group = lax.broadcasted_iota(jnp.int32, (ROWS, BLK), 1) // GROUP
    flipped = rows.T
    out = []
    for i in range(LANE_GROUPS):
        merged = None
        for g in range(LANE_GROUPS):
            piece = flipped[g * ROWS:(g + 1) * ROWS]
            shift = (g - i) * GROUP % BLK
            moved = pltpu.roll(piece, shift, 1) if shift else piece
            merged = moved if g == 0 else jnp.where(lane_group == g, moved, merged)
        out.append(merged)
    return out


def lane_steps():
    shape = (2 * BLK, STEPS * BLK)
    row = lax.broadcasted_iota(jnp.int32, shape, 0)
    col = lax.broadcasted_iota(jnp.int32, shape, 1)
    group = (col % BLK) // GROUP + col // BLK + 1
    block = col % GROUP + group // LANE_GROUPS
    group = group % LANE_GROUPS
    inside = (row == group * GROUP + block) & (block < ROWS)
    beyond = (row // GROUP == LANE_GROUPS + group) & (block == ROWS)
    return jnp.where(inside | beyond, 1.0, 0.0).astype(BF)


def kernel(
    fb, mask_in, delays_in, readers_in, stretch_in,
    series, stacked,
    fb_v, mask, stretch, delays_v, readers_v, delays_all, delays_s, readers_all,
    for_core, from_core, staged, parts, halo_f, halo_v, halo_all, sub_all, steps, reach,
    table, turned, rows, first, gathered, first_all, tall, grouped, outgoing, arrived,
    small_sem, load_sem, core_send, core_recv, part_send, part_recv,
    sub_send, sub_recv, halo_send, halo_recv, delay_send, delay_recv, delay_in,
    reader_send, reader_recv, row_send, row_recv, first_send, first_recv, out_send, out_recv,
):
    t, c = lax.axis_index("tm"), lax.axis_index("chan")
    core, me = t % 2, t // 2
    other = t + 1 - 2 * core
    x, q = t // NQ, t % NQ

    small = [
        pltpu.make_async_copy(source, target, small_sem.at[i])
        for i, (source, target) in enumerate(
            ((mask_in, mask), (delays_in, delays_v), (readers_in, readers_v), (stretch_in, stretch))
        )
    ]
    for copy in small:
        copy.start()

    def shard_at(n, parity):
        return 2 * ((me + 1 + n) % PAIRS) + parity

    def load(n, parity, slot):
        at = pl.ds(pl.multiple_of(shard_at(n, parity) * SHARD, SHARD), SHARD)
        return pltpu.make_async_copy(fb.at[:, at], fb_v.at[:, at], load_sem.at[slot])

    def start_other(n, carry):
        load(n, 1 - core, n).start()
        return carry

    def start_own(n, carry):
        load(n, core, PAIRS + n).start()
        return carry

    lax.fori_loop(0, PAIRS, start_other, 0)
    lax.fori_loop(0, PAIRS, start_own, 0)

    barrier = pltpu.get_barrier_semaphore()

    def greet(tm, chan):
        pl.semaphore_signal(barrier, inc=1, device_id=(tm, chan), device_id_type=MESH)

    def greet_plane(n, carry):
        greet((t + 1 + n) % N_TM, c)
        return carry

    lax.fori_loop(0, N_TM - 1, greet_plane, 0)
    for step in range(1, N_CHAN):
        greet(t, (c + step) % N_CHAN)

    @pl.when(t > 0)
    def _():
        for step in range(1, N_CHAN):
            greet(t - 1, (c + step) % N_CHAN)

    @pl.when(t < N_TM - 1)
    def _():
        for step in range(1, N_CHAN):
            greet(t + 1, (c + step) % N_CHAN)

    for copy in small:
        copy.wait()
    sublane = lax.broadcasted_iota(jnp.int32, (8, BLK), 0)
    weights = []
    for half in range(2):
        value = jnp.zeros((8, BLK), F32)
        for i in range(8):
            value = jnp.where(sublane == i, mask[8 * half + i].astype(F32), value)
        weights.append(value)

    def block_sum(at):
        block = fb_v[:, pl.ds(at, BLK)].astype(F32)
        return block[:8] * weights[0] + block[8:] * weights[1]

    def merge(blocks):
        step = 1
        while len(blocks) > 1:
            even = (sublane // step) % 2 == 0
            blocks = [
                jnp.where(even, a, b) + pltpu.roll(jnp.where(even, b, a), 8 - step, 0)
                for a, b in zip(blocks[0::2], blocks[1::2])
            ]
            step *= 2
        return blocks[0]

    def shard_sum(shard):
        base = pl.multiple_of(shard * SHARD, SHARD)
        return jnp.concatenate(
            [
                merge([block_sum(base + (8 * group + i) * BLK) for i in range(8)])
                for group in range(ROWS // 8)
            ],
            axis=0,
        )

    def to_core(chunk):
        at = pl.ds(chunk * CHUNK, CHUNK)
        return remote(
            for_core.at[at], from_core.at[at],
            core_send.at[chunk], core_recv.at[chunk], other, c,
        )

    pl.semaphore_wait(
        barrier,
        N_TM - 1 + N_CHAN - 1
        + (N_CHAN - 1) * ((t > 0).astype(jnp.int32) + (t < N_TM - 1).astype(jnp.int32)),
    )

    def delay_copy(step):
        return remote(
            delays_v, delays_all.at[c], delay_send.at[step - 1], delay_recv.at[c],
            t, (c + step) % N_CHAN,
        )

    def reader_copy(step):
        return remote(
            readers_v, readers_all.at[x], reader_send.at[step - 1], reader_recv.at[x],
            ((x + step) % NX) * NQ + q, c,
        )

    for step in range(1, N_CHAN):
        delay_copy(step).start()
    for step in range(1, NX):
        reader_copy(step).start()
    delays_all[c] = delays_v[...]
    readers_all[x] = readers_v[...]

    def sum_other(chunk, carry):
        for i in range(CHUNK):
            n = chunk * CHUNK + i
            load(n, 1 - core, n).wait()
            for_core[n] = shard_sum(shard_at(n, 1 - core))
        to_core(chunk).start()
        return carry

    lax.fori_loop(0, PAIRS // CHUNK, sum_other, 0)

    def send_part(n):
        return remote(
            staged.at[n], parts.at[me], part_send.at[n], part_recv.at[me],
            shard_at(n, core), c,
        )

    def sum_own(chunk, carry):
        to_core(chunk).wait_recv()
        for i in range(CHUNK):
            n = chunk * CHUNK + i
            load(n, core, PAIRS + n).wait()
            staged[n] = (shard_sum(shard_at(n, core)) + from_core[n]).astype(BF)

            @pl.when(n < PAIRS - 1)
            def _():
                send_part(n).start()

        return carry

    lax.fori_loop(0, PAIRS // CHUNK, sum_own, 0)
    parts[me] = staged[PAIRS - 1]

    def one_table(a, carry):
        table[a] = sinc_table(stretch[a])
        return carry

    lax.fori_loop(0, NACC, one_table, 0)
    steps[...] = lane_steps()
    halo_f[...] = jnp.zeros_like(halo_f)
    for step in range(1, N_CHAN):
        source = (c + step) % N_CHAN
        remote(
            delays_v, delays_all.at[source], delay_send.at[0], delay_recv.at[source], t, source
        ).wait_recv()
    delay_local = pltpu.make_async_copy(delays_all, delays_s, delay_in)
    delay_local.start()
    for step in range(1, NX):
        source = (x + step) % NX
        remote(
            readers_v, readers_all.at[source], reader_send.at[0], reader_recv.at[source],
            source * NQ + q, c,
        ).wait_recv()
    names = jnp.concatenate([readers_all[source][:, 0, :] for source in range(NX)], axis=1)
    reader_row = lax.broadcasted_iota(jnp.int32, (NQ, BLK), 0) + x * NQ
    pick = jnp.concatenate(
        [(names[a:a + 1] == reader_row).astype(F32) for a in range(NACC)], axis=0
    ).astype(BF)
    delay_local.wait()

    def part_arrival(j):
        return remote(parts.at[j], parts.at[j], part_send.at[0], part_recv.at[j], other, c)

    for stack in range(OWN // LANE_GROUPS):
        blocks = []
        for i in range(LANE_GROUPS):
            k = stack * LANE_GROUPS + i
            for j in (2 * k, 2 * k + 1):
                @pl.when(j != me)
                def _():
                    part_arrival(j).wait_recv()
            total = parts[2 * k].astype(F32) + parts[2 * k + 1].astype(F32)
            halo_f[k:k + 1] = total[:1]
            blocks.append(total)
        sub_all[c, stack * BLK:(stack + 1) * BLK] = turn(blocks).astype(BF)

    def sub_copy(step):
        return remote(
            sub_all.at[c], sub_all.at[c], sub_send.at[step - 1], sub_recv.at[c],
            t, (c + step) % N_CHAN,
        )

    def halo_copy(chan):
        return remote(
            halo_v, halo_all.at[c], halo_send.at[chan], halo_recv.at[c], t - 1, chan
        )

    for step in (2, 1, 3):
        sub_copy(step).start()
    first_blocks = halo_f[...]
    halo_v[...] = jnp.concatenate(
        [first_blocks] + [pltpu.roll(first_blocks, BLK - g * GROUP, 1) for g in range(1, LANE_GROUPS)],
        axis=0,
    ).T[:GROUP].astype(BF)

    @pl.when(t > 0)
    def _():
        for chan in range(N_CHAN):
            halo_copy(chan).start()

    @pl.when(t == N_TM - 1)
    def _():
        halo_all[...] = jnp.zeros_like(halo_all)

    @pl.when(t < N_TM - 1)
    def _():
        for chan in range(N_CHAN):
            remote(
                halo_v, halo_all.at[chan], halo_send.at[0], halo_recv.at[chan], t + 1, chan
            ).wait_recv()

    lane = lax.broadcasted_iota(jnp.int32, (GROUP, BLK), 1)
    totals = tuple(jnp.zeros((GROUP, BLK), F32) for _ in range(TRIALS))
    for step in (0, 1, 3, 2):
        source = (c + step) % N_CHAN
        if step:
            remote(
                sub_all.at[source], sub_all.at[source], sub_send.at[0], sub_recv.at[source],
                t, source,
            ).wait_recv()
        beyond = halo_all[source].astype(F32)

        def extend(k, carry):
            at = pl.ds(pl.multiple_of(k * GROUP, GROUP), GROUP)
            own = sub_all[source, at]
            next_blocks = jnp.where(lane % GROUP == k, beyond, 0.0).astype(BF)
            moved = jnp.dot(
                jnp.concatenate([own, next_blocks], axis=1), steps[...],
                preferred_element_type=F32,
            )
            reach[k, :GROUP] = own.astype(F32)
            for e in range(STEPS):
                reach[k, (e + 1) * GROUP:(e + 2) * GROUP] = moved[:, e * BLK:(e + 1) * BLK]
            return carry

        lax.fori_loop(0, OWN, extend, 0, unroll=4)

        def one_band(k, sums):
            return tuple(
                sums[m] + reach[k, pl.ds(delays_s[source, k, c * TRIALS + m], GROUP)]
                for m in range(TRIALS)
            )

        totals = lax.fori_loop(0, OWN, one_band, totals)

    for pair in range(TRIALS // LANE_GROUPS):
        back = turn_back(
            jnp.concatenate(totals[pair * LANE_GROUPS:(pair + 1) * LANE_GROUPS], axis=0)
        )
        for i in range(LANE_GROUPS):
            m = pair * LANE_GROUPS + i
            rows[m * ROWS:(m + 1) * ROWS] = back[i].astype(BF)
            turned[pl.ds(m, ROWS, stride=TRIALS)] = back[i]
    first[...] = jnp.concatenate([turned[:TRIALS], jnp.zeros((TRIALS, BLK), F32)], axis=0).astype(BF)

    def row_copy(step):
        return remote(
            rows, gathered.at[x], row_send.at[step - 1], row_recv.at[x],
            ((x + step) % NX) * NQ + q, c,
        )

    def first_copy(target):
        return remote(
            first, first_all.at[(t - 1) // NQ], first_send.at[target],
            first_recv.at[(t - 1) // NQ], target * NQ + (t - 1) % NQ, c,
        )

    for step in (2, 1, 3):
        row_copy(step).start()

    @pl.when(t > 0)
    def _():
        for target in range(NX):
            first_copy(target).start()

    gathered[x] = rows[...]
    for b in range(ROWS):
        series[:, b * BLK:(b + 1) * BLK] = turned[b * TRIALS:(b + 1) * TRIALS].astype(BF)

    def first_arrival(source):
        return remote(
            first, first_all.at[source], first_send.at[0], first_recv.at[source],
            source * NQ + q + 1, c,
        )

    for source in range(NX - 1):
        first_arrival(source).wait_recv()

    @pl.when(q < NQ - 1)
    def _():
        first_arrival(NX - 1).wait_recv()

    @pl.when(q == NQ - 1)
    def _():
        first_all[NX - 1] = jnp.zeros((16, BLK), BF)

    for step in range(1, NX):
        source = (x + step) % NX
        remote(
            rows, gathered.at[source], row_send.at[0], row_recv.at[source],
            source * NQ + q, c,
        ).wait_recv()

    for source in range(NX):
        last = first_all[source].astype(F32)
        for m in range(TRIALS):
            tall[m, source, :ROWS] = gathered[source, m * ROWS:(m + 1) * ROWS].astype(F32)
            tall[m, source, ROWS:ROWS + 1] = last[m:m + 1]
    for m in range(TRIALS):
        for half in range(2):
            block = jnp.concatenate(
                [tall[m, source, half:half + ROWS] for source in range(NX)], axis=0
            ).astype(BF)
            sums = jnp.dot(pick, block, preferred_element_type=F32)
            for a in range(NACC):
                grouped[a, half, pl.ds(m, NQ, stride=TRIALS)] = sums[a * NQ:(a + 1) * NQ]

    def two_accelerations(pair, carry):
        results = []
        for i in range(2):
            a = 2 * pair + i
            block = jnp.concatenate([grouped[a, 0], grouped[a, 1]], axis=1).astype(BF)
            results.append(jnp.dot(block, table[a], preferred_element_type=F32))
        for reader in range(NQ):
            at = slice(reader * TRIALS, (reader + 1) * TRIALS)
            outgoing[reader, pl.ds(pl.multiple_of(pair * 16, 16), 16)] = jnp.concatenate(
                [results[0][at], results[1][at]], axis=0
            ).astype(BF)
        return carry

    lax.fori_loop(0, NACC // 2, two_accelerations, 0)

    def out_copy(step):
        target = (q + step) % NQ
        return remote(
            outgoing.at[target], arrived.at[q], out_send.at[step - 1], out_recv.at[q],
            x * NQ + target, c,
        )

    for step in range(1, NQ):
        out_copy(step).start()
    total = outgoing[q].astype(F32)
    for step in range(1, NQ):
        source = (q + step) % NQ
        remote(
            outgoing.at[0], arrived.at[source], out_send.at[0], out_recv.at[source],
            x * NQ + source, c,
        ).wait_recv()
        total = total + arrived[source].astype(F32)
    for a in range(NACC):
        stacked[a] = total[a * TRIALS:(a + 1) * TRIALS].astype(BF)

    def sent_core(chunk, carry):
        to_core(chunk).wait_send()
        return carry

    def sent_part(n, carry):
        send_part(n).wait_send()
        return carry

    lax.fori_loop(0, PAIRS // CHUNK, sent_core, 0)
    lax.fori_loop(0, PAIRS - 1, sent_part, 0)
    for step in range(1, N_CHAN):
        delay_copy(step).wait_send()
        sub_copy(step).wait_send()
    for step in range(1, NX):
        reader_copy(step).wait_send()
        row_copy(step).wait_send()

    @pl.when(t > 0)
    def _():
        for chan in range(N_CHAN):
            halo_copy(chan).wait_send()
        for target in range(NX):
            first_copy(target).wait_send()

    for step in range(1, NQ):
        out_copy(step).wait_send()


def on_device(filterbank, channel_mask, delays, readers, stretch):
    hbm = pl.BlockSpec(memory_space=pltpu.HBM)
    vmem = pl.BlockSpec(memory_space=pltpu.VMEM)
    dma = pltpu.SemaphoreType.DMA
    return pl.pallas_call(
        kernel,
        out_shape=(
            jax.ShapeDtypeStruct((TRIALS, SHARD), BF),
            jax.ShapeDtypeStruct((NACC, TRIALS, BLK), BF),
        ),
        in_specs=[hbm] * 5,
        out_specs=(vmem, vmem),
        scratch_shapes=[
            pltpu.VMEM(filterbank.shape, BF),
            pltpu.SMEM((OWN,), jnp.int32),
            pltpu.SMEM((NACC,), F32),
            pltpu.VMEM((OWN, N_CHAN * TRIALS), jnp.int32),
            pltpu.VMEM((NACC, 1, ROWS), jnp.int32),
            pltpu.VMEM((N_CHAN, OWN, N_CHAN * TRIALS), jnp.int32),
            pltpu.SMEM((N_CHAN, OWN, N_CHAN * TRIALS), jnp.int32),
            pltpu.VMEM((NX, NACC, 1, ROWS), jnp.int32),
            pltpu.VMEM((PAIRS, ROWS, BLK), F32),
            pltpu.VMEM((PAIRS, ROWS, BLK), F32),
            pltpu.VMEM((PAIRS, ROWS, BLK), BF),
            pltpu.VMEM((PAIRS, ROWS, BLK), BF),
            pltpu.VMEM((ROWS, BLK), F32),
            pltpu.VMEM((GROUP, BLK), BF),
            pltpu.VMEM((N_CHAN, GROUP, BLK), BF),
            pltpu.VMEM((N_CHAN, OWN * GROUP, BLK), BF),
            pltpu.VMEM((2 * BLK, STEPS * BLK), BF),
            pltpu.VMEM((OWN, REACH, BLK), F32),
            pltpu.VMEM((NACC, 2 * BLK, BLK), BF),
            pltpu.VMEM((TRIALS * ROWS, BLK), F32),
            pltpu.VMEM((TRIALS * ROWS, BLK), BF),
            pltpu.VMEM((16, BLK), BF),
            pltpu.VMEM((NX, TRIALS * ROWS, BLK), BF),
            pltpu.VMEM((NX, 16, BLK), BF),
            pltpu.VMEM((TRIALS, NX, ROWS + 8, BLK), F32),
            pltpu.VMEM((NACC, 2, TRIALS * NQ, BLK), F32),
            pltpu.VMEM((NQ, NACC * TRIALS, BLK), BF),
            pltpu.VMEM((NQ, NACC * TRIALS, BLK), BF),
            dma((4,)),
            dma((N_TM,)),
            dma((PAIRS // CHUNK,)),
            dma((PAIRS // CHUNK,)),
            dma((PAIRS,)),
            dma((PAIRS,)),
        ]
        + [dma((N_CHAN,))] * 6
        + [dma]
        + [dma((NX,))] * 6
        + [dma((NQ,))] * 2,
        compiler_params=pltpu.CompilerParams(
            collective_id=0, has_side_effects=True, vmem_limit_bytes=60 * 2**20
        ),
        name="dedisperse",
    )(
        filterbank, channel_mask, delays.T, jnp.transpose(readers, (1, 2, 0)), stretch
    )


def solution(mesh):
    return jax.shard_map(
        on_device,
        mesh=mesh,
        in_specs=(
            P(("chan", "tm"), None),
            P(("chan", "tm")),
            P(None, "chan"),
            P("tm", None, None),
            P(),
        ),
        out_specs=(P("chan", "tm"), P(None, "chan", "tm")),
        check_vma=False,
    )
```

time: 78.9 us -> 58.9 us (0.75)
  Pallas kernels: 72.6 us -> 55.3 us
  local copies, waits for them, and re-layouts: 5.51 us -> 2.8 us
    pallas_call x3 -> x1, Pallas kernels: 72.6 us -> 55.3 us  [on_device(): pl.pallas_call(kernel, out_shape=(jax.ShapeDtypeStruct((TRIALS, SHARD), B...]
    unnamed x11 -> x2, local copies, waits for them, and re-layouts: 5.51 us -> 2.8 us
where the time goes in v2:
time: 58.9 us; the launch traced here: 58.8 us
  Pallas kernels  55.3 us (94%)
  local copies, waits for them, and re-layouts  2.8 us (5%)
  between operations  0.64 us (1%)
    pallas_call x1, Pallas kernels, on_device(): pl.pallas_call(kernel, out_shape=(jax.ShapeDtypeStruct((TRIALS, SHARD), B...  55.3 us
    unnamed x2, local copies, waits for them, and re-layouts  2.8 us

profile of v2, /device:TPU:1, one launch (start us, length us, event | category | flops | bytes accessed | tf_op | source)
XLA Modules:
  0.0 58.8 jit_solution(2239457483494473686)
XLA Ops:
  0.6 55.3 %dedisperse.1 = (bf16[8,4096]{1,0:T(8,128)(2,1)}, bf16[8,8,128]{2,1,0:T(8,128)(2,1)}) custom-call(bf16[16,262144]{1,0:T(8,128)(2,1)} %fb.1, s32[16]{0:T(128)} %mask_in.1, s32[16,32]{1,0:T(8,128)} %bitcast.2, s32[8,1,32]{2,1,0:T(1,128)} %bitcast.3, f32[8]{0:T(128)} %stretch_in.1), custom_call_target="tpu_custom_call" | custom-call | tf_op jit(solution)/shard_map/dedisperse/pallas_call | solution.py:522
  56.0 1.5 %copy.9 = bf16[8,4096]{1,0:T(8,128)(2,1)} copy(bf16[8,4096]{1,0:T(8,128)(2,1)} %get-tuple-element.4) | data formatting | bytes 131072
  57.4 1.3 %copy.10 = bf16[8,8,128]{2,1,0:T(8,128)(2,1)} copy(bf16[8,8,128]{2,1,0:T(8,128)(2,1)} %get-tuple-element.5) | data formatting | bytes 32768

commit v3 on v2

v3 whole, which is shorter than its diff:
```python
import math

import jax
import jax.numpy as jnp
from jax import lax
from jax.experimental import pallas as pl
from jax.experimental.pallas import tpu as pltpu
from jax.sharding import PartitionSpec as P

MESH = pl.DeviceIdType.MESH
BF, F32 = jnp.bfloat16, jnp.float32

BLK = 128
N_TM = 64
N_CHAN = 4
SHARD = 4096
ROWS = SHARD // BLK
PAIRS = N_TM // 2
OWN = 16
TRIALS = 8
NX = 4
NQ = 16
NZ = 8
FAR_Z = (4, 3, 5, 2, 6, 1, 7, 0)
NACC = 8
GROUP = 32
LANE_GROUPS = BLK // GROUP
STACKS = OWN // LANE_GROUPS
STEPS = 4
REACH = GROUP * (STEPS + 1)
CHUNK = 4
START_OFFSET = 4.0
TAPER_HALF = 8.0


def remote(src, dst, send_sem, recv_sem, tm, chan):
    return pltpu.make_async_remote_copy(
        src_ref=src,
        dst_ref=dst,
        send_sem=send_sem,
        recv_sem=recv_sem,
        device_id=(tm, chan),
        device_id_type=MESH,
    )


def sinc_tables(stretch, table):
    row = lax.broadcasted_iota(jnp.int32, (8, BLK), 0)
    col = lax.broadcasted_iota(jnp.int32, (8, BLK), 1).astype(F32)
    factor = jnp.zeros((8, BLK), F32)
    for a in range(NACC):
        factor = jnp.where(row == a, stretch[a], factor)
    centres = START_OFFSET + col * factor
    whole = jnp.round(centres)
    odd = whole - 2.0 * jnp.floor(whole * 0.5)
    waves = (2.0 * odd - 1.0) * jnp.sin(math.pi * (centres - whole)) / math.pi
    angle = (math.pi / TAPER_HALF) * (centres - 16.0 * jnp.floor(centres / 16.0))
    cosines, sines = 0.5 * jnp.cos(angle), 0.5 * jnp.sin(angle)
    sign = (1 - 2 * (row % 2)).astype(F32)
    turns = [(math.pi / TAPER_HALF) * (row + 8 * half).astype(F32) for half in range(2)]
    turns = [(jnp.cos(angle), jnp.sin(angle)) for angle in turns]
    for a in range(NACC):
        centre, wave, cos_p, sin_p = (
            jnp.broadcast_to(part[a:a + 1], (8, BLK)) for part in (centres, waves, cosines, sines)
        )
        wave = sign * wave
        tapers = [0.5 + cos_j * cos_p + sin_j * sin_p for cos_j, sin_j in turns]
        pieces = []
        for group in range(2 * BLK // 8):
            x = (row + 8 * group).astype(F32) - centre
            sinc = jnp.where(x == 0.0, 1.0, wave / jnp.where(x == 0.0, 1.0, x))
            pieces.append(jnp.where(jnp.abs(x) < TAPER_HALF, sinc * tapers[group % 2], 0.0))
        table[a] = jnp.concatenate(pieces, axis=0).astype(BF)


def turn(blocks):
    lane_group = lax.broadcasted_iota(jnp.int32, (ROWS, BLK), 1) // GROUP
    stacked = []
    for g in range(LANE_GROUPS):
        merged = blocks[0]
        for i in range(LANE_GROUPS):
            shift = (i - g) * GROUP % BLK
            moved = pltpu.roll(blocks[i], shift, 1) if shift else blocks[i]
            merged = moved if i == 0 else jnp.where(lane_group == i, moved, merged)
        stacked.append(merged)
    return jnp.concatenate(stacked, axis=0).T


def turn_back(rows):
    lane_group = lax.broadcasted_iota(jnp.int32, (ROWS, BLK), 1) // GROUP
    flipped = rows.T
    out = []
    for i in range(LANE_GROUPS):
        merged = None
        for g in range(LANE_GROUPS):
            piece = flipped[g * ROWS:(g + 1) * ROWS]
            shift = (g - i) * GROUP % BLK
            moved = pltpu.roll(piece, shift, 1) if shift else piece
            merged = moved if g == 0 else jnp.where(lane_group == g, moved, merged)
        out.append(merged)
    return out


def lane_steps():
    shape = (2 * BLK, STEPS * BLK)
    row = lax.broadcasted_iota(jnp.int32, shape, 0)
    col = lax.broadcasted_iota(jnp.int32, shape, 1)
    group = (col % BLK) // GROUP + col // BLK + 1
    block = col % GROUP + group // LANE_GROUPS
    group = group % LANE_GROUPS
    inside = (row == group * GROUP + block) & (block < ROWS)
    beyond = (row // GROUP == LANE_GROUPS + group) & (block == ROWS)
    return jnp.where(inside | beyond, 1.0, 0.0).astype(BF)


def kernel(
    fb, mask_in, delays_in, readers_in, stretch_in,
    series_out, arrived,
    series, fb_v, mask, stretch, delays, readers_v, readers_all,
    for_core, own_sum, from_core, staged, parts,
    for_first, own_first, from_first, next_row, next_parts, halo_f,
    trials_out, trials_in, steps, reach,
    table, turned, rows, first, gathered, first_all, tall, grouped,
    outgoing, from_half, leaving,
    small_sem, result_sem, load_sem, core_send, core_recv, part_send, part_recv,
    first_core_sem, next_send, next_recv, trial_send, trial_recv,
    reader_send, reader_recv, row_send, row_recv, first_send, first_recv,
    half_send, half_recv, out_send, out_recv, own_sem,
):
    t, c = lax.axis_index("tm"), lax.axis_index("chan")
    core, me = lax.rem(t, 2), t // 2
    other = t + 1 - 2 * core
    x, q = t // NQ, lax.rem(t, NQ)
    z = q // 2

    small = [
        pltpu.make_async_copy(source, target, small_sem.at[i])
        for i, (source, target) in enumerate(
            ((mask_in, mask), (delays_in, delays), (readers_in, readers_v), (stretch_in, stretch))
        )
    ]
    for copy in small:
        copy.start()

    turn_side = 1 - 2 * core

    def chip_at(chunk, i, parity):
        half, g = chunk // 4, lax.rem(chunk, 4)
        dx = 2 - g + 3 * (g // 2) - 2 * (g // 3)
        dz = FAR_Z[i] + half * (FAR_Z[CHUNK + i] - FAR_Z[i])
        side = 1 - 2 * parity
        return NZ * lax.rem(x + NX + side * dx, NX) + lax.rem(z + NZ + side * dz, NZ)

    def load(n):
        at = pl.ds(pl.multiple_of(n * 2 * SHARD, 2 * SHARD), 2 * SHARD)
        return pltpu.make_async_copy(fb.at[:, at], fb_v.at[:, at], load_sem.at[n])

    def start_load(n, carry):
        load(n).start()
        return carry

    def greet_plane(n, carry):
        greet(lax.rem(t + n, N_TM), c)
        return carry

    def greet(tm, chan):
        pl.semaphore_signal(barrier, inc=1, device_id=(tm, chan), device_id_type=MESH)

    barrier = pltpu.get_barrier_semaphore()
    lax.fori_loop(0, 8, start_load, 0)
    lax.fori_loop(24, 48, greet_plane, 0)
    lax.fori_loop(8, PAIRS, start_load, 0)
    lax.fori_loop(1, 24, greet_plane, 0)
    lax.fori_loop(48, N_TM, greet_plane, 0)
    for step in range(1, N_CHAN):
        greet(t, lax.rem(c + step, N_CHAN))

    for copy in small:
        copy.wait()
    sublane = lax.broadcasted_iota(jnp.int32, (8, BLK), 0)
    weights = []
    for half in range(2):
        value = jnp.zeros((8, BLK), F32)
        for i in range(8):
            value = jnp.where(sublane == i, mask[8 * half + i].astype(F32), value)
        weights.append(value)

    def block_sum(at):
        block = fb_v[:, pl.ds(at, BLK)].astype(F32)
        return block[:8] * weights[0] + block[8:] * weights[1]

    def merge(blocks):
        step = 1
        while len(blocks) > 1:
            even = (sublane // step) % 2 == 0
            blocks = [
                jnp.where(even, a, b) + pltpu.roll(jnp.where(even, b, a), 8 - step, 0)
                for a, b in zip(blocks[0::2], blocks[1::2])
            ]
            step *= 2
        return blocks[0]

    def shard_sum(shard):
        base = pl.multiple_of(shard * SHARD, SHARD)
        return jnp.concatenate(
            [
                merge([block_sum(base + (8 * group + i) * BLK) for i in range(8)])
                for group in range(ROWS // 8)
            ],
            axis=0,
        )

    to_core = remote(for_core, from_core, core_send, core_recv, other, c)

    def sum_chip(n, carry):
        load(n).wait()
        for_core[n] = shard_sum(2 * n + 1 - core)
        own_sum[n] = shard_sum(2 * n + core)
        for_first[pl.ds(n, 1)] = for_core[n, :1]
        own_first[pl.ds(n, 1)] = own_sum[n, :1]
        return carry

    lax.fori_loop(0, PAIRS, sum_chip, 0)
    pl.semaphore_wait(barrier, N_TM - 1 + N_CHAN - 1)

    first_to_core = remote(
        own_first, from_first, first_core_sem.at[0], first_core_sem.at[1], other, c
    )

    to_core.start()
    first_to_core.start()

    def reader_copy(step):
        return remote(
            readers_v, readers_all.at[x], reader_send.at[step - 1], reader_recv.at[x],
            lax.rem(x + step, NX) * NQ + q, c,
        )

    for step in range(1, NX):
        reader_copy(step).start()
    readers_all[x] = readers_v[...]

    def send_part(chunk, i):
        chip = chip_at(chunk, i, core)
        return remote(
            staged.at[chip], parts.at[me], part_send, part_recv,
            2 * chip + core, c,
        )

    to_core.wait_recv()

    def send_parts(chunk, carry):
        for i in range(CHUNK):
            chip = chip_at(chunk, i, core)
            staged[chip] = (own_sum[chip] + from_core[chip]).astype(BF)
            if i < CHUNK - 1:
                send_part(chunk, i).start()
            else:
                @pl.when(chunk < PAIRS // CHUNK - 1)
                def _():
                    send_part(chunk, i).start()

        return carry

    def send_next(chunk, i):
        chip = chip_at(chunk, i, core)
        return remote(
            next_row.at[chip + core], next_parts.at[me], next_send, next_recv,
            2 * chip + core, c,
        )

    def send_nexts(chunk, carry):
        for i in range(CHUNK):
            if i < CHUNK - 1:
                send_next(chunk, i).start()
            else:
                @pl.when(chunk < PAIRS // CHUNK - 1)
                def _():
                    send_next(chunk, i).start()

        return carry

    lax.fori_loop(0, PAIRS // CHUNK, send_parts, 0)
    first_to_core.wait_recv()
    next_row[PAIRS:] = jnp.zeros((1, 1, BLK), F32)
    next_row[:PAIRS] = (for_first[...] + from_first[...]).reshape(PAIRS, 1, BLK)
    lax.fori_loop(0, PAIRS // CHUNK, send_nexts, 0)
    parts[me] = staged[me]
    next_parts[me] = next_row[me + core]

    sinc_tables(stretch, table)
    steps[...] = lane_steps()
    halo_f[...] = jnp.zeros_like(halo_f)
    for step in range(1, NX):
        source = lax.rem(x + step, NX)
        remote(
            readers_v, readers_all.at[source], reader_send.at[0], reader_recv.at[source],
            source * NQ + q, c,
        ).wait_recv()
    names = jnp.concatenate([readers_all[source][:, 0, :] for source in range(NX)], axis=1)
    reader_row = lax.broadcasted_iota(jnp.int32, (NQ, BLK), 0) + x * NQ
    pick = jnp.concatenate(
        [(names[a:a + 1] == reader_row).astype(F32) for a in range(NACC)], axis=0
    ).astype(BF)

    others = pl.ds(0, PAIRS - 1)
    all_parts = remote(parts.at[others], parts.at[others], part_send, part_recv, other, c)
    all_nexts = remote(
        next_parts.at[others], next_parts.at[others], next_send, next_recv, other, c
    )
    all_parts.wait_recv()
    own = []
    for stack in range(STACKS):
        blocks = []
        for k in range(stack * LANE_GROUPS, (stack + 1) * LANE_GROUPS):
            blocks.append(parts[2 * k].astype(F32) + parts[2 * k + 1].astype(F32))
        own.append(turn(blocks).astype(BF))
    own = jnp.concatenate(own, axis=0)
    reach[:, :GROUP] = own.astype(F32).reshape(OWN, GROUP, BLK)

    all_nexts.wait_recv()
    for k in range(OWN):
        halo_f[k:k + 1] = next_parts[2 * k] + next_parts[2 * k + 1]
    first_blocks = halo_f[...]
    beyond = jnp.concatenate(
        [first_blocks] + [pltpu.roll(first_blocks, BLK - g * GROUP, 1) for g in range(1, LANE_GROUPS)],
        axis=0,
    ).T[:GROUP]
    lane = lax.broadcasted_iota(jnp.int32, (GROUP, BLK), 1)
    next_blocks = jnp.concatenate(
        [jnp.where(lane % GROUP == k, beyond, 0.0).astype(BF) for k in range(OWN)], axis=0
    )
    both = jnp.concatenate([own, next_blocks], axis=1)
    for pair in range(STEPS // 2):
        moved = jnp.dot(
            both, steps[:, pair * 2 * BLK:(pair + 1) * 2 * BLK], preferred_element_type=F32
        )
        for i in range(2):
            e = 2 * pair + i + 1
            reach[:, e * GROUP:(e + 1) * GROUP] = moved[:, i * BLK:(i + 1) * BLK].reshape(
                OWN, GROUP, BLK
            )

    def trials_of(chan):
        def one_band(k, sums):
            return tuple(
                sums[m] + reach[k, pl.ds(delays[k, chan * TRIALS + m], GROUP)]
                for m in range(TRIALS)
            )

        return lax.fori_loop(
            0, OWN, one_band, tuple(jnp.zeros((GROUP, BLK), F32) for _ in range(TRIALS))
        )

    def chan_at(step):
        return lax.rem(c + N_CHAN + turn_side * step, N_CHAN)

    def trial_copy(step):
        return remote(
            trials_out.at[step - 1], trials_in.at[c], trial_send.at[step - 1], trial_recv.at[c],
            t, chan_at(step),
        )

    for step in (2, 1, 3):
        sums = trials_of(chan_at(step))
        trials_out[step - 1] = jnp.concatenate(sums, axis=0).astype(BF)
        trial_copy(step).start()
    totals = jnp.concatenate(trials_of(c), axis=0)
    to_core.wait_send()
    first_to_core.wait_send()
    all_parts.wait_send()
    all_nexts.wait_send()
    for step in range(1, NX):
        reader_copy(step).wait_send()
    for step in (1, 3, 2):
        source = chan_at(step)
        remote(
            trials_out.at[0], trials_in.at[source], trial_send.at[0], trial_recv.at[source],
            t, source,
        ).wait_recv()
        totals = totals + trials_in[source].astype(F32)

    def row_copy(half, step):
        return remote(
            rows.at[half], gathered.at[x, half], row_send.at[half, step - 1], row_recv.at[half, x],
            lax.rem(x + NX + turn_side * step, NX) * NQ + q, c,
        )

    def first_copy(target):
        return remote(
            first, first_all.at[(t - 1) // NQ], first_send.at[target],
            first_recv.at[(t - 1) // NQ], target * NQ + lax.rem(t - 1, NQ), c,
        )

    backs = []
    for pair in range(TRIALS // LANE_GROUPS):
        backs += turn_back(totals[pair * BLK:(pair + 1) * BLK])
    first[...] = jnp.concatenate(
        [back[:1] for back in backs] + [jnp.zeros((TRIALS, BLK), F32)], axis=0
    ).astype(BF)

    @pl.when(t > 0)
    def _():
        for target in range(NX):
            first_copy(target).start()

    for half in range(2):
        for i in range(LANE_GROUPS):
            rows[half, i * ROWS:(i + 1) * ROWS] = backs[half * LANE_GROUPS + i].astype(BF)
        for step in (2, 1, 3):
            row_copy(half, step).start()
    gathered[x] = rows[...]
    for m in range(TRIALS):
        turned[pl.ds(m, ROWS, stride=TRIALS)] = backs[m]
    for b in range(ROWS):
        series[:, b * BLK:(b + 1) * BLK] = turned[b * TRIALS:(b + 1) * TRIALS].astype(BF)

    series_copy = pltpu.make_async_copy(series, series_out, result_sem)
    series_copy.start()

    for step in range(1, N_CHAN):
        trial_copy(step).wait_send()

    def first_arrival(source):
        return remote(
            first, first_all.at[source], first_send.at[0], first_recv.at[source],
            source * NQ + q + 1, c,
        )

    for step in (0, 1, 3, 2):
        source = lax.rem(x + step, NX)
        if step:
            for half in range(2):
                remote(
                    rows.at[half], gathered.at[source, half], row_send.at[half, 0],
                    row_recv.at[half, source], source * NQ + q, c,
                ).wait_recv()
        for m in range(TRIALS):
            at = m % LANE_GROUPS * ROWS
            tall[m, source, :ROWS] = gathered[source, m // LANE_GROUPS, at:at + ROWS].astype(F32)
    for step in (0, 1, 3, 2):
        source = lax.rem(x + step, NX)
        last_block = source * NQ + q == N_TM - 1

        @pl.when(jnp.logical_not(last_block))
        def _():
            first_arrival(source).wait_recv()

        @pl.when(last_block)
        def _():
            first_all[NX - 1] = jnp.zeros((16, BLK), BF)

        last = first_all[source].astype(F32)
        for m in range(TRIALS):
            tall[m, source, ROWS:ROWS + 1] = last[m:m + 1]

    for m in range(TRIALS):
        for half in range(2):
            block = jnp.concatenate(
                [tall[m, source, half:half + ROWS] for source in range(NX)], axis=0
            ).astype(BF)
            sums = jnp.dot(pick, block, preferred_element_type=F32)
            for a in range(NACC):
                grouped[a, half, pl.ds(m, NQ, stride=TRIALS)] = sums[a * NQ:(a + 1) * NQ]

    def half_copy(half):
        return remote(
            outgoing.at[1 - core, half], from_half.at[half], half_send.at[half], half_recv.at[half],
            other, c,
        )

    def z_at(n):
        return lax.rem(z + NZ + turn_side * FAR_Z[n], NZ)

    def out_copy(half, n):
        target = z_at(n)
        return remote(
            leaving.at[half, target], arrived.at[half, z],
            out_send.at[half], out_recv.at[half], x * NQ + 2 * target + core, c,
        )

    def sent_out(half):
        others = pl.ds(0, NZ - 1)
        return remote(
            leaving.at[half, others], arrived.at[half, others],
            out_send.at[half], out_recv.at[half], other, c,
        )

    def own_copy(half):
        return pltpu.make_async_copy(
            leaving.at[half, z], arrived.at[half, z], own_sem.at[half]
        )

    for half in range(2):
        for pair in range(2):
            results = []
            for i in range(2):
                a = 4 * half + 2 * pair + i
                block = jnp.concatenate([grouped[a, 0], grouped[a, 1]], axis=1).astype(BF)
                results.append(jnp.dot(block, table[a], preferred_element_type=F32))
            for reader in range(NQ):
                at = slice(reader * TRIALS, (reader + 1) * TRIALS)
                outgoing[reader % 2, half, reader // 2, pair * 16:(pair + 1) * 16] = (
                    jnp.concatenate([results[0][at], results[1][at]], axis=0)
                )
        half_copy(half).start()
    for half in range(2):
        half_copy(half).wait_recv()
        for n in range(NZ):
            target = z_at(n)
            leaving[half, target] = (outgoing[core, half, target] + from_half[half, target]).astype(BF)
            if n < NZ - 1:
                out_copy(half, n).start()
            else:
                own_copy(half).start()
    for step in range(1, NX):
        for half in range(2):
            row_copy(half, step).wait_send()

    @pl.when(t > 0)
    def _():
        for target in range(NX):
            first_copy(target).wait_send()

    for half in range(2):
        half_copy(half).wait_send()
    series_copy.wait()
    for half in range(2):
        sent_out(half).wait_recv()

    for half in range(2):
        sent_out(half).wait_send()
        own_copy(half).wait()


def finish(series_in, arrived, series, stacked):
    series[...] = series_in[...]
    for half in range(2):
        total = arrived[half, 0].astype(F32)
        for source in range(1, NZ):
            total = total + arrived[half, source].astype(F32)
        for i in range(NACC // 2):
            stacked[half * (NACC // 2) + i] = total[i * TRIALS:(i + 1) * TRIALS].astype(BF)


def on_device(filterbank, channel_mask, delays, readers, stretch):
    hbm = pl.BlockSpec(memory_space=pltpu.HBM)
    vmem = pl.BlockSpec(memory_space=pltpu.VMEM)
    dma = pltpu.SemaphoreType.DMA
    results = pl.pallas_call(
        kernel,
        out_shape=(
            jax.ShapeDtypeStruct((TRIALS, SHARD), BF),
            jax.ShapeDtypeStruct((2, NZ, NACC * TRIALS // 2, BLK), BF),
        ),
        in_specs=[hbm] * 5,
        out_specs=(hbm, hbm),
        scratch_shapes=[
            pltpu.VMEM((TRIALS, SHARD), BF),
            pltpu.VMEM(filterbank.shape, BF),
            pltpu.SMEM((OWN,), jnp.int32),
            pltpu.SMEM((NACC,), F32),
            pltpu.SMEM((OWN, N_CHAN * TRIALS), jnp.int32),
            pltpu.VMEM((NACC, 1, ROWS), jnp.int32),
            pltpu.VMEM((NX, NACC, 1, ROWS), jnp.int32),
            pltpu.VMEM((PAIRS, ROWS, BLK), F32),
            pltpu.VMEM((PAIRS, ROWS, BLK), F32),
            pltpu.VMEM((PAIRS, ROWS, BLK), F32),
            pltpu.VMEM((PAIRS, ROWS, BLK), BF),
            pltpu.VMEM((PAIRS, ROWS, BLK), BF),
            pltpu.VMEM((PAIRS, BLK), F32),
            pltpu.VMEM((PAIRS, BLK), F32),
            pltpu.VMEM((PAIRS, BLK), F32),
            pltpu.VMEM((PAIRS + 1, 1, BLK), F32),
            pltpu.VMEM((PAIRS, 1, BLK), F32),
            pltpu.VMEM((ROWS, BLK), F32),
            pltpu.VMEM((N_CHAN - 1, TRIALS * GROUP, BLK), BF),
            pltpu.VMEM((N_CHAN, TRIALS * GROUP, BLK), BF),
            pltpu.VMEM((2 * BLK, STEPS * BLK), BF),
            pltpu.VMEM((OWN, REACH, BLK), F32),
            pltpu.VMEM((NACC, 2 * BLK, BLK), BF),
            pltpu.VMEM((TRIALS * ROWS, BLK), F32),
            pltpu.VMEM((2, BLK, BLK), BF),
            pltpu.VMEM((16, BLK), BF),
            pltpu.VMEM((NX, 2, BLK, BLK), BF),
            pltpu.VMEM((NX, 16, BLK), BF),
            pltpu.VMEM((TRIALS, NX, ROWS + 8, BLK), F32),
            pltpu.VMEM((NACC, 2, TRIALS * NQ, BLK), F32),
            pltpu.VMEM((2, 2, NZ, NACC * TRIALS // 2, BLK), F32),
            pltpu.VMEM((2, NZ, NACC * TRIALS // 2, BLK), F32),
            pltpu.VMEM((2, NZ, NACC * TRIALS // 2, BLK), BF),
            dma((4,)),
            dma,
            dma((PAIRS,)),
            dma,
            dma,
            dma,
            dma,
            dma((2,)),
            dma,
            dma,
            dma((N_CHAN,)),
            dma((N_CHAN,)),
            dma((NX,)),
            dma((NX,)),
            dma((2, NX)),
            dma((2, NX)),
            dma((NX,)),
            dma((NX,)),
            dma((2,)),
            dma((2,)),
            dma((2,)),
            dma((2,)),
            dma((2,)),
        ],
        compiler_params=pltpu.CompilerParams(
            collective_id=0, has_side_effects=True, vmem_limit_bytes=60 * 2**20
        ),
        name="dedisperse",
    )(
        filterbank, channel_mask, delays.T, jnp.transpose(readers, (1, 2, 0)), stretch
    )
    return pl.pallas_call(
        finish,
        out_shape=(
            jax.ShapeDtypeStruct((TRIALS, SHARD), BF),
            jax.ShapeDtypeStruct((NACC, TRIALS, BLK), BF),
        ),
        in_specs=[vmem] * 2,
        out_specs=(vmem, vmem),
        compiler_params=pltpu.CompilerParams(vmem_limit_bytes=60 * 2**20),
        name="results",
    )(*results)


def solution(mesh):
    return jax.shard_map(
        on_device,
        mesh=mesh,
        in_specs=(
            P(("chan", "tm"), None),
            P(("chan", "tm")),
            P(None, "chan"),
            P("tm", None, None),
            P(),
        ),
        out_specs=(P("chan", "tm"), P(None, "chan", "tm")),
        check_vma=False,
    )
```

time: 58.9 us -> 46.6 us (0.79)
  Pallas kernels: 55.3 us -> 45.8 us
  local copies, waits for them, and re-layouts: 2.8 us -> 0 us
    pallas_call x1, Pallas kernels: 55.3 us -> 44.3 us  [on_device(): pl.pallas_call(kernel, out_shape=(jax.ShapeDtypeStruct((TRIALS, SHARD), B...]
    unnamed x2 -> x0, local copies, waits for them, and re-layouts: 2.8 us -> none
    pallas_call x0 -> x1, Pallas kernels: none -> 1.58 us  [on_device(): pl.pallas_call(finish, out_shape=(jax.ShapeDtypeStruct((TRIALS, SHARD), B...]
where the time goes in v3:
time: 46.6 us; the launch traced here: 46.5 us
  Pallas kernels  45.8 us (98%)
  between operations  0.64 us (1%)
    pallas_call x1, Pallas kernels, on_device(): pl.pallas_call(kernel, out_shape=(jax.ShapeDtypeStruct((TRIALS, SHARD), B...  44.3 us
    pallas_call x1, Pallas kernels, on_device(): pl.pallas_call(finish, out_shape=(jax.ShapeDtypeStruct((TRIALS, SHARD), B...  1.58 us

profile of v3, /device:TPU:1, one launch (start us, length us, event | category | flops | bytes accessed | tf_op | source)
XLA Modules:
  0.0 46.5 jit_solution(7852920719629383472)
XLA Ops:
  0.6 44.3 %dedisperse.1 = (bf16[8,4096]{1,0:T(8,128)(2,1)}, bf16[2,8,32,128]{3,2,1,0:T(8,128)(2,1)}) custom-call(bf16[16,262144]{1,0:T(8,128)(2,1)} %fb.1, s32[16]{0:T(128)} %mask_in.1, s32[16,32]{1,0:T(8,128)} %bitcast.2, s32[8,1,32]{2,1,0:T(1,128)} %bitcast.3, f32[8]{0:T(128)} %stretch_in.1), custom_call_target="tpu_custom_call" | custom-call | tf_op jit(solution)/shard_map/dedisperse/pallas_call | solution.py:550
  44.9 1.6 %results.1 = (bf16[8,4096]{1,0:T(8,128)(2,1)}, bf16[8,8,128]{2,1,0:T(8,128)(2,1)}) custom-call(bf16[8,4096]{1,0:T(8,128)(2,1)} %get-tuple-element.4.series_in, bf16[2,8,32,128]{3,2,1,0:T(8,128)(2,1)} %get-tuple-element.5.arrived), custom_call_target="tpu_custom_call" | custom-call | tf_op jit(solution)/shard_map/results/pallas_call | solution.py:623

commit v4 on v3

--- a/solution.py
+++ b/solution.py
@@ -18,9 +18,11 @@
 PAIRS = N_TM // 2
 OWN = 16
 TRIALS = 8
+HALF = TRIALS // 2
 NX = 4
 NQ = 16
 NZ = 8
+FAR_X = (2, 1, 3, 0)
 FAR_Z = (4, 3, 5, 2, 6, 1, 7, 0)
 NACC = 8
 GROUP = 32
@@ -145,8 +147,11 @@
     turn_side = 1 - 2 * core
 
     def chip_at(chunk, i, parity):
-        half, g = chunk // 4, lax.rem(chunk, 4)
-        dx = 2 - g + 3 * (g // 2) - 2 * (g // 3)
+        if isinstance(chunk, int):
+            half, dx = chunk // 4, FAR_X[chunk % 4]
+        else:
+            half, g = chunk // 4, lax.rem(chunk, 4)
+            dx = 2 - g + 3 * (g // 2) - 2 * (g // 3)
         dz = FAR_Z[i] + half * (FAR_Z[CHUNK + i] - FAR_Z[i])
         side = 1 - 2 * parity
         return NZ * lax.rem(x + NX + side * dx, NX) + lax.rem(z + NZ + side * dz, NZ)
@@ -210,7 +215,12 @@
             axis=0,
         )
 
-    to_core = remote(for_core, from_core, core_send, core_recv, other, c)
+    def to_core(row):
+        at = pl.ds(pl.multiple_of(row * NZ, NZ), NZ)
+        return remote(
+            for_core.at[at], from_core.at[at], core_send.at[row], core_recv.at[row], other, c
+        )
+
 
     def sum_chip(n, carry):
         load(n).wait()
@@ -227,8 +237,9 @@
         own_first, from_first, first_core_sem.at[0], first_core_sem.at[1], other, c
     )
 
-    to_core.start()
     first_to_core.start()
+    for g in range(NX):
+        to_core(lax.rem(x + NX - turn_side * FAR_X[g], NX)).start()
 
     def reader_copy(step):
         return remote(
@@ -246,19 +257,19 @@
             staged.at[chip], parts.at[me], part_send, part_recv,
             2 * chip + core, c,
         )
-
-    to_core.wait_recv()
 
     def send_parts(chunk, carry):
         for i in range(CHUNK):
             chip = chip_at(chunk, i, core)
             staged[chip] = (own_sum[chip] + from_core[chip]).astype(BF)
-            if i < CHUNK - 1:
+            if i < CHUNK - 1 or isinstance(chunk, int):
                 send_part(chunk, i).start()
+                send_next(chunk, i).start()
             else:
                 @pl.when(chunk < PAIRS // CHUNK - 1)
                 def _():
                     send_part(chunk, i).start()
+                    send_next(chunk, i).start()
 
         return carry
 
@@ -269,22 +280,14 @@
             2 * chip + core, c,
         )
 
-    def send_nexts(chunk, carry):
-        for i in range(CHUNK):
-            if i < CHUNK - 1:
-                send_next(chunk, i).start()
-            else:
-                @pl.when(chunk < PAIRS // CHUNK - 1)
-                def _():
-                    send_next(chunk, i).start()
-
-        return carry
-
-    lax.fori_loop(0, PAIRS // CHUNK, send_parts, 0)
     first_to_core.wait_recv()
     next_row[PAIRS:] = jnp.zeros((1, 1, BLK), F32)
     next_row[:PAIRS] = (for_first[...] + from_first[...]).reshape(PAIRS, 1, BLK)
-    lax.fori_loop(0, PAIRS // CHUNK, send_nexts, 0)
+
+    for chunk in range(NX):
+        to_core(lax.rem(x + NX + turn_side * FAR_X[chunk], NX)).wait_recv()
+        send_parts(chunk, 0)
+    lax.fori_loop(NX, PAIRS // CHUNK, send_parts, 0)
     parts[me] = staged[me]
     next_parts[me] = next_row[me + core]
 
@@ -341,44 +344,37 @@
                 OWN, GROUP, BLK
             )
 
-    def trials_of(chan):
+    def trials_of(chan, half):
         def one_band(k, sums):
             return tuple(
-                sums[m] + reach[k, pl.ds(delays[k, chan * TRIALS + m], GROUP)]
-                for m in range(TRIALS)
+                sums[m] + reach[k, pl.ds(delays[k, chan * TRIALS + half * HALF + m], GROUP)]
+                for m in range(HALF)
             )
 
-        return lax.fori_loop(
-            0, OWN, one_band, tuple(jnp.zeros((GROUP, BLK), F32) for _ in range(TRIALS))
-        )
+        sums = tuple(jnp.zeros((GROUP, BLK), F32) for _ in range(HALF))
+        return jnp.concatenate(lax.fori_loop(0, OWN, one_band, sums, unroll=2), axis=0)
 
     def chan_at(step):
         return lax.rem(c + N_CHAN + turn_side * step, N_CHAN)
 
-    def trial_copy(step):
-        return remote(
-            trials_out.at[step - 1], trials_in.at[c], trial_send.at[step - 1], trial_recv.at[c],
-            t, chan_at(step),
-        )
-
-    for step in (2, 1, 3):
-        sums = trials_of(chan_at(step))
-        trials_out[step - 1] = jnp.concatenate(sums, axis=0).astype(BF)
-        trial_copy(step).start()
-    totals = jnp.concatenate(trials_of(c), axis=0)
-    to_core.wait_send()
+    def trial_copy(half, step):
+        return remote(
+            trials_out.at[half, step - 1], trials_in.at[half, c],
+            trial_send.at[half, step - 1], trial_recv.at[half, c], t, chan_at(step),
+        )
+
+    for half in range(2):
+        for step in (2, 1, 3):
+            trials_out[half, step - 1] = trials_of(chan_at(step), half).astype(BF)
+            trial_copy(half, step).start()
+    totals = [trials_of(c, half) for half in range(2)]
+    for row in range(NX):
+        to_core(row).wait_send()
     first_to_core.wait_send()
     all_parts.wait_send()
     all_nexts.wait_send()
     for step in range(1, NX):
         reader_copy(step).wait_send()
-    for step in (1, 3, 2):
-        source = chan_at(step)
-        remote(
-            trials_out.at[0], trials_in.at[source], trial_send.at[0], trial_recv.at[source],
-            t, source,
-        ).wait_recv()
-        totals = totals + trials_in[source].astype(F32)
 
     def row_copy(half, step):
         return remote(
@@ -393,20 +389,28 @@
         )
 
     backs = []
-    for pair in range(TRIALS // LANE_GROUPS):
-        backs += turn_back(totals[pair * BLK:(pair + 1) * BLK])
-    first[...] = jnp.concatenate(
-        [back[:1] for back in backs] + [jnp.zeros((TRIALS, BLK), F32)], axis=0
-    ).astype(BF)
-
-    @pl.when(t > 0)
-    def _():
-        for target in range(NX):
-            first_copy(target).start()
-
-    for half in range(2):
-        for i in range(LANE_GROUPS):
-            rows[half, i * ROWS:(i + 1) * ROWS] = backs[half * LANE_GROUPS + i].astype(BF)
+    for half in range(2):
+        total = totals[half]
+        for step in (1, 3, 2):
+            source = chan_at(step)
+            remote(
+                trials_out.at[half, 0], trials_in.at[half, source],
+                trial_send.at[half, 0], trial_recv.at[half, source], t, source,
+            ).wait_recv()
+            total = total + trials_in[half, source].astype(F32)
+        backs += turn_back(total)
+        if half == 1:
+            first[...] = jnp.concatenate(
+                [back[:1] for back in backs] + [jnp.zeros((TRIALS, BLK), F32)], axis=0
+            ).astype(BF)
+
+            @pl.when(t > 0)
+            def _():
+                for target in range(NX):
+                    first_copy(target).start()
+
+        for i in range(HALF):
+            rows[half, i * ROWS:(i + 1) * ROWS] = backs[half * HALF + i].astype(BF)
         for step in (2, 1, 3):
             row_copy(half, step).start()
     gathered[x] = rows[...]
@@ -418,8 +422,9 @@
     series_copy = pltpu.make_async_copy(series, series_out, result_sem)
     series_copy.start()
 
-    for step in range(1, N_CHAN):
-        trial_copy(step).wait_send()
+    for half in range(2):
+        for step in range(1, N_CHAN):
+            trial_copy(half, step).wait_send()
 
     def first_arrival(source):
         return remote(
@@ -427,19 +432,25 @@
             source * NQ + q + 1, c,
         )
 
-    for step in (0, 1, 3, 2):
-        source = lax.rem(x + step, NX)
-        if step:
-            for half in range(2):
-                remote(
-                    rows.at[half], gathered.at[source, half], row_send.at[half, 0],
-                    row_recv.at[half, source], source * NQ + q, c,
-                ).wait_recv()
-        for m in range(TRIALS):
-            at = m % LANE_GROUPS * ROWS
-            tall[m, source, :ROWS] = gathered[source, m // LANE_GROUPS, at:at + ROWS].astype(F32)
-    for step in (0, 1, 3, 2):
-        source = lax.rem(x + step, NX)
+    def group(m, upper, block):
+        sums = jnp.dot(pick, block, preferred_element_type=F32)
+        for a in range(NACC):
+            grouped[a, upper, pl.ds(m, NQ, stride=TRIALS)] = sums[a * NQ:(a + 1) * NQ]
+
+    for half in range(2):
+        for step in (1, 3, 2):
+            source = lax.rem(x + step, NX)
+            remote(
+                rows.at[half], gathered.at[source, half], row_send.at[half, 0],
+                row_recv.at[half, source], source * NQ + q, c,
+            ).wait_recv()
+        for i in range(HALF):
+            m, at = half * HALF + i, i * ROWS
+            pieces = [gathered[source, half, at:at + ROWS] for source in range(NX)]
+            group(m, 0, jnp.concatenate(pieces, axis=0))
+            for source in range(NX):
+                tall[m, source, :ROWS] = pieces[source].astype(F32)
+    for source in range(NX):
         last_block = source * NQ + q == N_TM - 1
 
         @pl.when(jnp.logical_not(last_block))
@@ -448,20 +459,16 @@
 
         @pl.when(last_block)
         def _():
-            first_all[NX - 1] = jnp.zeros((16, BLK), BF)
+            first_all[source] = jnp.zeros((16, BLK), BF)
 
         last = first_all[source].astype(F32)
         for m in range(TRIALS):
             tall[m, source, ROWS:ROWS + 1] = last[m:m + 1]
-
     for m in range(TRIALS):
-        for half in range(2):
-            block = jnp.concatenate(
-                [tall[m, source, half:half + ROWS] for source in range(NX)], axis=0
-            ).astype(BF)
-            sums = jnp.dot(pick, block, preferred_element_type=F32)
-            for a in range(NACC):
-                grouped[a, half, pl.ds(m, NQ, stride=TRIALS)] = sums[a * NQ:(a + 1) * NQ]
+        group(
+            m, 1,
+            jnp.concatenate([tall[m, source, 1:1 + ROWS] for source in range(NX)], axis=0).astype(BF),
+        )
 
     def half_copy(half):
         return remote(
@@ -574,8 +581,8 @@
             pltpu.VMEM((PAIRS + 1, 1, BLK), F32),
             pltpu.VMEM((PAIRS, 1, BLK), F32),
             pltpu.VMEM((ROWS, BLK), F32),
-            pltpu.VMEM((N_CHAN - 1, TRIALS * GROUP, BLK), BF),
-            pltpu.VMEM((N_CHAN, TRIALS * GROUP, BLK), BF),
+            pltpu.VMEM((2, N_CHAN - 1, HALF * GROUP, BLK), BF),
+            pltpu.VMEM((2, N_CHAN, HALF * GROUP, BLK), BF),
             pltpu.VMEM((2 * BLK, STEPS * BLK), BF),
             pltpu.VMEM((OWN, REACH, BLK), F32),
             pltpu.VMEM((NACC, 2 * BLK, BLK), BF),
@@ -592,15 +599,15 @@
             dma((4,)),
             dma,
             dma((PAIRS,)),
-            dma,
-            dma,
+            dma((NX,)),
+            dma((NX,)),
             dma,
             dma,
             dma((2,)),
             dma,
             dma,
-            dma((N_CHAN,)),
-            dma((N_CHAN,)),
+            dma((2, N_CHAN)),
+            dma((2, N_CHAN)),
             dma((NX,)),
             dma((NX,)),
             dma((2, NX)),

time: 46.6 us -> 43.9 us (0.942)
  Pallas kernels: 45.8 us -> 43.1 us
    pallas_call x1, Pallas kernels: 44.3 us -> 41.5 us  [on_device(): pl.pallas_call(kernel, out_shape=(jax.ShapeDtypeStruct((TRIALS, SHARD), B...]
where the time goes in v4:
time: 43.9 us; the launch traced here: 43.8 us
  Pallas kernels  43.1 us (98%)
  between operations  0.64 us (1%)
    pallas_call x1, Pallas kernels, on_device(): pl.pallas_call(kernel, out_shape=(jax.ShapeDtypeStruct((TRIALS, SHARD), B...  41.5 us
    pallas_call x1, Pallas kernels, on_device(): pl.pallas_call(finish, out_shape=(jax.ShapeDtypeStruct((TRIALS, SHARD), B...  1.58 us

profile of v4, /device:TPU:1, one launch (start us, length us, event | category | flops | bytes accessed | tf_op | source)
XLA Modules:
  0.0 43.8 jit_solution(3164588316281414149)
XLA Ops:
  0.6 41.5 %dedisperse.1 = (bf16[8,4096]{1,0:T(8,128)(2,1)}, bf16[2,8,32,128]{3,2,1,0:T(8,128)(2,1)}) custom-call(bf16[16,262144]{1,0:T(8,128)(2,1)} %fb.1, s32[16]{0:T(128)} %mask_in.1, s32[16,32]{1,0:T(8,128)} %bitcast.2, s32[8,1,32]{2,1,0:T(1,128)} %bitcast.3, f32[8]{0:T(128)} %stretch_in.1), custom_call_target="tpu_custom_call" | custom-call | tf_op jit(solution)/shard_map/dedisperse/pallas_call | solution.py:557
  42.2 1.6 %results.1 = (bf16[8,4096]{1,0:T(8,128)(2,1)}, bf16[8,8,128]{2,1,0:T(8,128)(2,1)}) custom-call(bf16[8,4096]{1,0:T(8,128)(2,1)} %get-tuple-element.4.series_in, bf16[2,8,32,128]{3,2,1,0:T(8,128)(2,1)} %get-tuple-element.5.arrived), custom_call_target="tpu_custom_call" | custom-call | tf_op jit(solution)/shard_map/results/pallas_call | solution.py:630

commit v5 on v4

--- a/solution.py
+++ b/solution.py
@@ -226,8 +226,8 @@
         load(n).wait()
         for_core[n] = shard_sum(2 * n + 1 - core)
         own_sum[n] = shard_sum(2 * n + core)
-        for_first[pl.ds(n, 1)] = for_core[n, :1]
-        own_first[pl.ds(n, 1)] = own_sum[n, :1]
+        for_first[n] = for_core[n, :1]
+        own_first[n] = own_sum[n, :1]
         return carry
 
     lax.fori_loop(0, PAIRS, sum_chip, 0)
@@ -247,8 +247,6 @@
             lax.rem(x + step, NX) * NQ + q, c,
         )
 
-    for step in range(1, NX):
-        reader_copy(step).start()
     readers_all[x] = readers_v[...]
 
     def send_part(chunk, i):
@@ -282,12 +280,14 @@
 
     first_to_core.wait_recv()
     next_row[PAIRS:] = jnp.zeros((1, 1, BLK), F32)
-    next_row[:PAIRS] = (for_first[...] + from_first[...]).reshape(PAIRS, 1, BLK)
+    next_row[:PAIRS] = for_first[...] + from_first[...]
 
     for chunk in range(NX):
         to_core(lax.rem(x + NX + turn_side * FAR_X[chunk], NX)).wait_recv()
         send_parts(chunk, 0)
     lax.fori_loop(NX, PAIRS // CHUNK, send_parts, 0)
+    for step in range(1, NX):
+        reader_copy(step).start()
     parts[me] = staged[me]
     next_parts[me] = next_row[me + core]
 
@@ -382,10 +382,10 @@
             lax.rem(x + NX + turn_side * step, NX) * NQ + q, c,
         )
 
-    def first_copy(target):
-        return remote(
-            first, first_all.at[(t - 1) // NQ], first_send.at[target],
-            first_recv.at[(t - 1) // NQ], target * NQ + lax.rem(t - 1, NQ), c,
+    def first_copy(half, target):
+        return remote(
+            first.at[half], first_all.at[half, (t - 1) // NQ], first_send.at[half, target],
+            first_recv.at[half, (t - 1) // NQ], target * NQ + lax.rem(t - 1, NQ), c,
         )
 
     backs = []
@@ -398,19 +398,19 @@
                 trial_send.at[half, 0], trial_recv.at[half, source], t, source,
             ).wait_recv()
             total = total + trials_in[half, source].astype(F32)
-        backs += turn_back(total)
-        if half == 1:
-            first[...] = jnp.concatenate(
-                [back[:1] for back in backs] + [jnp.zeros((TRIALS, BLK), F32)], axis=0
-            ).astype(BF)
-
-            @pl.when(t > 0)
-            def _():
-                for target in range(NX):
-                    first_copy(target).start()
+        back = turn_back(total)
+        backs += back
+        first[half] = jnp.concatenate(
+            [block[:1] for block in back] + [jnp.zeros((16 - HALF, BLK), F32)], axis=0
+        ).astype(BF)
+
+        @pl.when(t > 0)
+        def _():
+            for target in range(NX):
+                first_copy(half, target).start()
 
         for i in range(HALF):
-            rows[half, i * ROWS:(i + 1) * ROWS] = backs[half * HALF + i].astype(BF)
+            rows[half, i * ROWS:(i + 1) * ROWS] = back[i].astype(BF)
         for step in (2, 1, 3):
             row_copy(half, step).start()
     gathered[x] = rows[...]
@@ -426,48 +426,10 @@
         for step in range(1, N_CHAN):
             trial_copy(half, step).wait_send()
 
-    def first_arrival(source):
-        return remote(
-            first, first_all.at[source], first_send.at[0], first_recv.at[source],
-            source * NQ + q + 1, c,
-        )
-
-    def group(m, upper, block):
-        sums = jnp.dot(pick, block, preferred_element_type=F32)
-        for a in range(NACC):
-            grouped[a, upper, pl.ds(m, NQ, stride=TRIALS)] = sums[a * NQ:(a + 1) * NQ]
-
-    for half in range(2):
-        for step in (1, 3, 2):
-            source = lax.rem(x + step, NX)
-            remote(
-                rows.at[half], gathered.at[source, half], row_send.at[half, 0],
-                row_recv.at[half, source], source * NQ + q, c,
-            ).wait_recv()
-        for i in range(HALF):
-            m, at = half * HALF + i, i * ROWS
-            pieces = [gathered[source, half, at:at + ROWS] for source in range(NX)]
-            group(m, 0, jnp.concatenate(pieces, axis=0))
-            for source in range(NX):
-                tall[m, source, :ROWS] = pieces[source].astype(F32)
-    for source in range(NX):
-        last_block = source * NQ + q == N_TM - 1
-
-        @pl.when(jnp.logical_not(last_block))
-        def _():
-            first_arrival(source).wait_recv()
-
-        @pl.when(last_block)
-        def _():
-            first_all[source] = jnp.zeros((16, BLK), BF)
-
-        last = first_all[source].astype(F32)
-        for m in range(TRIALS):
-            tall[m, source, ROWS:ROWS + 1] = last[m:m + 1]
-    for m in range(TRIALS):
-        group(
-            m, 1,
-            jnp.concatenate([tall[m, source, 1:1 + ROWS] for source in range(NX)], axis=0).astype(BF),
+    def first_arrival(half, source):
+        return remote(
+            first.at[half], first_all.at[half, source], first_send.at[half, 0],
+            first_recv.at[half, source], source * NQ + q + 1, c,
         )
 
     def half_copy(half):
@@ -498,20 +460,7 @@
             leaving.at[half, z], arrived.at[half, z], own_sem.at[half]
         )
 
-    for half in range(2):
-        for pair in range(2):
-            results = []
-            for i in range(2):
-                a = 4 * half + 2 * pair + i
-                block = jnp.concatenate([grouped[a, 0], grouped[a, 1]], axis=1).astype(BF)
-                results.append(jnp.dot(block, table[a], preferred_element_type=F32))
-            for reader in range(NQ):
-                at = slice(reader * TRIALS, (reader + 1) * TRIALS)
-                outgoing[reader % 2, half, reader // 2, pair * 16:(pair + 1) * 16] = (
-                    jnp.concatenate([results[0][at], results[1][at]], axis=0)
-                )
-        half_copy(half).start()
-    for half in range(2):
+    def send_out(half):
         half_copy(half).wait_recv()
         for n in range(NZ):
             target = z_at(n)
@@ -520,14 +469,65 @@
                 out_copy(half, n).start()
             else:
                 own_copy(half).start()
+
+    def group(i, upper, block):
+        sums = jnp.dot(pick, block, preferred_element_type=F32)
+        for a in range(NACC):
+            grouped[a, upper, pl.ds(i, NQ, stride=HALF)] = sums[a * NQ:(a + 1) * NQ]
+
+    for half in range(2):
+        for step in (1, 3, 2):
+            source = lax.rem(x + step, NX)
+            remote(
+                rows.at[half], gathered.at[source, half], row_send.at[half, 0],
+                row_recv.at[half, source], source * NQ + q, c,
+            ).wait_recv()
+        if half == 1:
+            send_out(0)
+        for i in range(HALF):
+            at = i * ROWS
+            pieces = [gathered[source, half, at:at + ROWS] for source in range(NX)]
+            group(i, 0, jnp.concatenate(pieces, axis=0))
+            for source in range(NX):
+                tall[i, source, :ROWS] = pieces[source].astype(F32)
+        for source in range(NX):
+            last_block = source * NQ + q == N_TM - 1
+
+            @pl.when(jnp.logical_not(last_block))
+            def _():
+                first_arrival(half, source).wait_recv()
+
+            @pl.when(last_block)
+            def _():
+                first_all[half, source] = jnp.zeros((16, BLK), BF)
+
+            last = first_all[half, source].astype(F32)
+            for i in range(HALF):
+                tall[i, source, ROWS:ROWS + 1] = last[i:i + 1]
+        for i in range(HALF):
+            pieces = [tall[i, source, 1:1 + ROWS] for source in range(NX)]
+            group(i, 1, jnp.concatenate(pieces, axis=0).astype(BF))
+        for pair in range(NACC // 2):
+            results = []
+            for a in (2 * pair, 2 * pair + 1):
+                block = jnp.concatenate([grouped[a, 0], grouped[a, 1]], axis=1).astype(BF)
+                results.append(jnp.dot(block, table[a], preferred_element_type=F32))
+            for reader in range(NQ):
+                at = slice(reader * HALF, (reader + 1) * HALF)
+                outgoing[reader % 2, half, reader // 2, pair * 8:(pair + 1) * 8] = (
+                    jnp.concatenate([results[0][at], results[1][at]], axis=0)
+                )
+        half_copy(half).start()
+    send_out(1)
     for step in range(1, NX):
         for half in range(2):
             row_copy(half, step).wait_send()
 
     @pl.when(t > 0)
     def _():
-        for target in range(NX):
-            first_copy(target).wait_send()
+        for half in range(2):
+            for target in range(NX):
+                first_copy(half, target).wait_send()
 
     for half in range(2):
         half_copy(half).wait_send()
@@ -542,12 +542,15 @@
 
 def finish(series_in, arrived, series, stacked):
     series[...] = series_in[...]
+    halves = []
     for half in range(2):
         total = arrived[half, 0].astype(F32)
         for source in range(1, NZ):
             total = total + arrived[half, source].astype(F32)
-        for i in range(NACC // 2):
-            stacked[half * (NACC // 2) + i] = total[i * TRIALS:(i + 1) * TRIALS].astype(BF)
+        halves.append(total)
+    for a in range(NACC):
+        at = slice(a * HALF, (a + 1) * HALF)
+        stacked[a] = jnp.concatenate([total[at] for total in halves], axis=0).astype(BF)
 
 
 def on_device(filterbank, channel_mask, delays, readers, stretch):
@@ -575,9 +578,9 @@
             pltpu.VMEM((PAIRS, ROWS, BLK), F32),
             pltpu.VMEM((PAIRS, ROWS, BLK), BF),
             pltpu.VMEM((PAIRS, ROWS, BLK), BF),
-            pltpu.VMEM((PAIRS, BLK), F32),
-            pltpu.VMEM((PAIRS, BLK), F32),
-            pltpu.VMEM((PAIRS, BLK), F32),
+            pltpu.VMEM((PAIRS, 1, BLK), F32),
+            pltpu.VMEM((PAIRS, 1, BLK), F32),
+            pltpu.VMEM((PAIRS, 1, BLK), F32),
             pltpu.VMEM((PAIRS + 1, 1, BLK), F32),
             pltpu.VMEM((PAIRS, 1, BLK), F32),
             pltpu.VMEM((ROWS, BLK), F32),
@@ -588,11 +591,11 @@
             pltpu.VMEM((NACC, 2 * BLK, BLK), BF),
             pltpu.VMEM((TRIALS * ROWS, BLK), F32),
             pltpu.VMEM((2, BLK, BLK), BF),
-            pltpu.VMEM((16, BLK), BF),
+            pltpu.VMEM((2, 16, BLK), BF),
             pltpu.VMEM((NX, 2, BLK, BLK), BF),
-            pltpu.VMEM((NX, 16, BLK), BF),
-            pltpu.VMEM((TRIALS, NX, ROWS + 8, BLK), F32),
-            pltpu.VMEM((NACC, 2, TRIALS * NQ, BLK), F32),
+            pltpu.VMEM((2, NX, 16, BLK), BF),
+            pltpu.VMEM((HALF, NX, ROWS + 8, BLK), F32),
+            pltpu.VMEM((NACC, 2, HALF * NQ, BLK), F32),
             pltpu.VMEM((2, 2, NZ, NACC * TRIALS // 2, BLK), F32),
             pltpu.VMEM((2, NZ, NACC * TRIALS // 2, BLK), F32),
             pltpu.VMEM((2, NZ, NACC * TRIALS // 2, BLK), BF),
@@ -612,8 +615,8 @@
             dma((NX,)),
             dma((2, NX)),
             dma((2, NX)),
-            dma((NX,)),
-            dma((NX,)),
+            dma((2, NX)),
+            dma((2, NX)),
             dma((2,)),
             dma((2,)),
             dma((2,)),

time: 43.9 us -> 43.2 us (0.984)
  Pallas kernels: 43.1 us -> 42.4 us
    pallas_call x1, Pallas kernels: 41.5 us -> 40.8 us  [on_device(): pl.pallas_call(kernel, out_shape=(jax.ShapeDtypeStruct((TRIALS, SHARD), B...]
where the time goes in v5:
time: 43.2 us; the launch traced here: 43.1 us
  Pallas kernels  42.4 us (98%)
  between operations  0.64 us (1%)
    pallas_call x1, Pallas kernels, on_device(): pl.pallas_call(kernel, out_shape=(jax.ShapeDtypeStruct((TRIALS, SHARD), B...  40.8 us
    pallas_call x1, Pallas kernels, on_device(): pl.pallas_call(finish, out_shape=(jax.ShapeDtypeStruct((TRIALS, SHARD), B...  1.58 us

profile of v5, /device:TPU:1, one launch (start us, length us, event | category | flops | bytes accessed | tf_op | source)
XLA Modules:
  0.0 43.1 jit_solution(3012883778855755933)
XLA Ops:
  0.6 40.8 %dedisperse.1 = (bf16[8,4096]{1,0:T(8,128)(2,1)}, bf16[2,8,32,128]{3,2,1,0:T(8,128)(2,1)}) custom-call(bf16[16,262144]{1,0:T(8,128)(2,1)} %fb.1, s32[16]{0:T(128)} %mask_in.1, s32[16,32]{1,0:T(8,128)} %bitcast.2, s32[8,1,32]{2,1,0:T(1,128)} %bitcast.3, f32[8]{0:T(128)} %stretch_in.1), custom_call_target="tpu_custom_call" | custom-call | tf_op jit(solution)/shard_map/dedisperse/pallas_call | solution.py:560
  41.5 1.6 %results.1 = (bf16[8,4096]{1,0:T(8,128)(2,1)}, bf16[8,8,128]{2,1,0:T(8,128)(2,1)}) custom-call(bf16[8,4096]{1,0:T(8,128)(2,1)} %get-tuple-element.4.series_in, bf16[2,8,32,128]{3,2,1,0:T(8,128)(2,1)} %get-tuple-element.5.arrived), custom_call_target="tpu_custom_call" | custom-call | tf_op jit(solution)/shard_map/results/pallas_call | solution.py:633

commit v6 on v5

--- a/solution.py
+++ b/solution.py
@@ -23,6 +23,7 @@
 NQ = 16
 NZ = 8
 FAR_X = (2, 1, 3, 0)
+OWN_CHIP = (7, 3)
 FAR_Z = (4, 3, 5, 2, 6, 1, 7, 0)
 NACC = 8
 GROUP = 32
@@ -147,12 +148,7 @@
     turn_side = 1 - 2 * core
 
     def chip_at(chunk, i, parity):
-        if isinstance(chunk, int):
-            half, dx = chunk // 4, FAR_X[chunk % 4]
-        else:
-            half, g = chunk // 4, lax.rem(chunk, 4)
-            dx = 2 - g + 3 * (g // 2) - 2 * (g // 3)
-        dz = FAR_Z[i] + half * (FAR_Z[CHUNK + i] - FAR_Z[i])
+        dx, dz = FAR_X[chunk % NX], FAR_Z[chunk // NX * CHUNK + i]
         side = 1 - 2 * parity
         return NZ * lax.rem(x + NX + side * dx, NX) + lax.rem(z + NZ + side * dz, NZ)
 
@@ -164,6 +160,12 @@
         load(n).start()
         return carry
 
+    def row_at(g):
+        return lax.rem(x + FAR_X[g], NX)
+
+    def start_row(g):
+        lax.fori_loop(row_at(g) * NZ, row_at(g) * NZ + NZ, start_load, 0)
+
     def greet_plane(n, carry):
         greet(lax.rem(t + n, N_TM), c)
         return carry
@@ -172,9 +174,11 @@
         pl.semaphore_signal(barrier, inc=1, device_id=(tm, chan), device_id_type=MESH)
 
     barrier = pltpu.get_barrier_semaphore()
-    lax.fori_loop(0, 8, start_load, 0)
-    lax.fori_loop(24, 48, greet_plane, 0)
-    lax.fori_loop(8, PAIRS, start_load, 0)
+    lax.fori_loop(24, 32, greet_plane, 0)
+    start_row(0)
+    lax.fori_loop(32, 48, greet_plane, 0)
+    for g in range(1, NX):
+        start_row(g)
     lax.fori_loop(1, 24, greet_plane, 0)
     lax.fori_loop(48, N_TM, greet_plane, 0)
     for step in range(1, N_CHAN):
@@ -230,16 +234,22 @@
         own_first[n] = own_sum[n, :1]
         return carry
 
-    lax.fori_loop(0, PAIRS, sum_chip, 0)
+    def sum_row(g):
+        lax.fori_loop(row_at(g) * NZ, row_at(g) * NZ + NZ, sum_chip, 0)
+
+    for g in range(NX - 1):
+        sum_row(g)
     pl.semaphore_wait(barrier, N_TM - 1 + N_CHAN - 1)
 
     first_to_core = remote(
         own_first, from_first, first_core_sem.at[0], first_core_sem.at[1], other, c
     )
 
+    for g in range(NX - 1):
+        to_core(lax.rem(x + NX - turn_side * FAR_X[g], NX)).start()
+    sum_row(NX - 1)
     first_to_core.start()
-    for g in range(NX):
-        to_core(lax.rem(x + NX - turn_side * FAR_X[g], NX)).start()
+    to_core(x).start()
 
     def reader_copy(step):
         return remote(
@@ -256,20 +266,14 @@
             2 * chip + core, c,
         )
 
-    def send_parts(chunk, carry):
+    def send_parts(chunk):
         for i in range(CHUNK):
             chip = chip_at(chunk, i, core)
             staged[chip] = (own_sum[chip] + from_core[chip]).astype(BF)
-            if i < CHUNK - 1 or isinstance(chunk, int):
+            if (chunk, i) != OWN_CHIP:
                 send_part(chunk, i).start()
-                send_next(chunk, i).start()
-            else:
-                @pl.when(chunk < PAIRS // CHUNK - 1)
-                def _():
-                    send_part(chunk, i).start()
+                if chunk:
                     send_next(chunk, i).start()
-
-        return carry
 
     def send_next(chunk, i):
         chip = chip_at(chunk, i, core)
@@ -278,14 +282,16 @@
             2 * chip + core, c,
         )
 
-    first_to_core.wait_recv()
-    next_row[PAIRS:] = jnp.zeros((1, 1, BLK), F32)
-    next_row[:PAIRS] = for_first[...] + from_first[...]
-
-    for chunk in range(NX):
-        to_core(lax.rem(x + NX + turn_side * FAR_X[chunk], NX)).wait_recv()
-        send_parts(chunk, 0)
-    lax.fori_loop(NX, PAIRS // CHUNK, send_parts, 0)
+    for chunk in range(PAIRS // CHUNK):
+        if chunk < NX:
+            to_core(lax.rem(x + NX + turn_side * FAR_X[chunk], NX)).wait_recv()
+        send_parts(chunk)
+        if chunk == 0:
+            first_to_core.wait_recv()
+            next_row[PAIRS:] = jnp.zeros((1, 1, BLK), F32)
+            next_row[:PAIRS] = for_first[...] + from_first[...]
+            for i in range(CHUNK):
+                send_next(chunk, i).start()
     for step in range(1, NX):
         reader_copy(step).start()
     parts[me] = staged[me]

time: 43.2 us -> 42.8 us (level)
  no operation moved by 1% of the time
where the time goes in v6:
time: 42.8 us; the launch traced here: 42.7 us
  Pallas kernels  42.1 us (98%)
  between operations  0.64 us (1%)
    pallas_call x1, Pallas kernels, on_device(): pl.pallas_call(kernel, out_shape=(jax.ShapeDtypeStruct((TRIALS, SHARD), B...  40.5 us
    pallas_call x1, Pallas kernels, on_device(): pl.pallas_call(finish, out_shape=(jax.ShapeDtypeStruct((TRIALS, SHARD), B...  1.58 us

profile of v6, /device:TPU:1, one launch (start us, length us, event | category | flops | bytes accessed | tf_op | source)
XLA Modules:
  0.0 42.7 jit_solution(9814685583426443260)
XLA Ops:
  0.6 40.5 %dedisperse.1 = (bf16[8,4096]{1,0:T(8,128)(2,1)}, bf16[2,8,32,128]{3,2,1,0:T(8,128)(2,1)}) custom-call(bf16[16,262144]{1,0:T(8,128)(2,1)} %fb.1, s32[16]{0:T(128)} %mask_in.1, s32[16,32]{1,0:T(8,128)} %bitcast.2, s32[8,1,32]{2,1,0:T(1,128)} %bitcast.3, f32[8]{0:T(128)} %stretch_in.1), custom_call_target="tpu_custom_call" | custom-call | tf_op jit(solution)/shard_map/dedisperse/pallas_call | solution.py:566
  41.1 1.6 %results.1 = (bf16[8,4096]{1,0:T(8,128)(2,1)}, bf16[8,8,128]{2,1,0:T(8,128)(2,1)}) custom-call(bf16[8,4096]{1,0:T(8,128)(2,1)} %get-tuple-element.4.series_in, bf16[2,8,32,128]{3,2,1,0:T(8,128)(2,1)} %get-tuple-element.5.arrived), custom_call_target="tpu_custom_call" | custom-call | tf_op jit(solution)/shard_map/results/pallas_call | solution.py:639

commit v7 on v5

--- a/solution.py
+++ b/solution.py
@@ -404,15 +404,20 @@
             [block[:1] for block in back] + [jnp.zeros((16 - HALF, BLK), F32)], axis=0
         ).astype(BF)
 
-        @pl.when(t > 0)
-        def _():
-            for target in range(NX):
-                first_copy(half, target).start()
-
+        def send_first():
+            @pl.when(t > 0)
+            def _():
+                for target in range(NX):
+                    first_copy(half, target).start()
+
+        if half == 1:
+            send_first()
         for i in range(HALF):
             rows[half, i * ROWS:(i + 1) * ROWS] = back[i].astype(BF)
         for step in (2, 1, 3):
             row_copy(half, step).start()
+        if half == 0:
+            send_first()
     gathered[x] = rows[...]
     for m in range(TRIALS):
         turned[pl.ds(m, ROWS, stride=TRIALS)] = backs[m]

time: 43.2 us -> 43.2 us (level)
  no operation moved by 1% of the time
where the time goes in v7:
time: 43.2 us; the launch traced here: 43.1 us
  Pallas kernels  42.5 us (98%)
  between operations  0.64 us (1%)
    pallas_call x1, Pallas kernels, on_device(): pl.pallas_call(kernel, out_shape=(jax.ShapeDtypeStruct((TRIALS, SHARD), B...  40.9 us
    pallas_call x1, Pallas kernels, on_device(): pl.pallas_call(finish, out_shape=(jax.ShapeDtypeStruct((TRIALS, SHARD), B...  1.58 us

profile of v7, /device:TPU:1, one launch (start us, length us, event | category | flops | bytes accessed | tf_op | source)
XLA Modules:
  0.0 43.1 jit_solution(11303684566955685950)
XLA Ops:
  0.6 40.9 %dedisperse.1 = (bf16[8,4096]{1,0:T(8,128)(2,1)}, bf16[2,8,32,128]{3,2,1,0:T(8,128)(2,1)}) custom-call(bf16[16,262144]{1,0:T(8,128)(2,1)} %fb.1, s32[16]{0:T(128)} %mask_in.1, s32[16,32]{1,0:T(8,128)} %bitcast.2, s32[8,1,32]{2,1,0:T(1,128)} %bitcast.3, f32[8]{0:T(128)} %stretch_in.1), custom_call_target="tpu_custom_call" | custom-call | tf_op jit(solution)/shard_map/dedisperse/pallas_call | solution.py:565
  41.5 1.6 %results.1 = (bf16[8,4096]{1,0:T(8,128)(2,1)}, bf16[8,8,128]{2,1,0:T(8,128)(2,1)}) custom-call(bf16[8,4096]{1,0:T(8,128)(2,1)} %get-tuple-element.4.series_in, bf16[2,8,32,128]{3,2,1,0:T(8,128)(2,1)} %get-tuple-element.5.arrived), custom_call_target="tpu_custom_call" | custom-call | tf_op jit(solution)/shard_map/results/pallas_call | solution.py:638
